TPU v7x, 256 devices: a whole 4x4x8 slice. The times are simulated.
256 devices in a mesh: subdomai: 8 (over x, core), inner: 32 (over z, y).
Axes of the slice: x: 4, y: 4, z: 8, core: 2. Of those that a mesh axis runs over, the one named last changes fastest.
Arguments:
- start_vectors: float32 [8, 4096, 64, 128], P(None, ('subdomai', 'inner')), may hold values from -6 to 6
- permeability: float32 [4096, 64, 128], P(('subdomai', 'inner')), may hold values from 0.01 to 100
- accumulation: float32 [4096, 64, 128], P(('subdomai', 'inner')), may hold values from 0.1 to 2
- extents: int32 [8, 2], P('subdomai'), may hold values from 2 to 512, as said below
- neighbour_ids: int32 [8, 6], P('subdomai'), may hold values from 0 to 7, as said below
- intersection_widths: int32 [8, 6], P('subdomai'), may hold values from 1 to 4, as said below
Outputs:
- coarse_basis: float32 [8, 4096, 64, 128], P(None, ('subdomai', 'inner'))
- galerkin: float32 [8, 8, 8], P('subdomai')
- coupling: float32 [8, 6, 8, 8], P('subdomai')
Inputs may be any that keep to these rules, and one draw needn't show every extreme that they name: extents[i] = (first-dimension extent in 2 to 512, third-dimension extent in 4 to 128); in every draw some subdomain is active in full. `neighbour_ids`: each row lists 6 different subdomains other than its own. `intersection_widths`: 4 is reached in every draw.
All inputs are finite; a program needn't handle non-finite values.
Results may differ from a plain program's by a relative error of at most 0.0003.
Values sent between devices are 32-bit elements; how exact they have to be, the bound alone decides.
No kernel may reach another device: no remote copies, remote signals or barrier semaphores. Data moves between devices by JAX's collectives and lax.ppermute only.
A program may use at most 192 MiB of HBM per device.

v0:
```python
import jax
import jax.numpy as jnp
from jax import lax
from jax.sharding import PartitionSpec as P

WMAX = 4
CY = 64
CZ = 128


omega = 0.6


def padded(x, sides, width):
    for axis, dim in sides:
        devices, length = (lax.axis_size(axis), x.shape[dim])
        up = [(i, (i + 1) % devices) for i in range(devices - 1)]
        down = [(j, i) for i, j in up]
        last = lax.slice_in_dim(x, length - width, length, axis=dim)
        initial = lax.slice_in_dim(x, 0, width, axis=dim)
        before = lax.ppermute(last, axis, up)
        after = lax.ppermute(initial, axis, down)
        x = jnp.concatenate([before, x, after], axis=dim)
    return x


def face_terms(perm_pad, mask_pad, axis):
    count = perm_pad.shape[axis]
    first = lax.slice_in_dim(perm_pad, 0, count - 1, axis=axis)
    second = lax.slice_in_dim(perm_pad, 1, count, axis=axis)
    mfirst = lax.slice_in_dim(mask_pad, 0, count - 1, axis=axis)
    msecond = lax.slice_in_dim(mask_pad, 1, count, axis=axis)
    return mfirst * msecond * 2.0 * first * second / (first + second)


def coefficients(perm_xpad, mask_xpad, accum):
    perm = perm_xpad[1:-1]
    mask = mask_xpad[1:-1]
    along_x = face_terms(perm_xpad, mask_xpad, 0)
    along_y = face_terms(
        jnp.pad(perm, ((0, 0), (1, 1), (0, 0))), jnp.pad(mask, ((0, 0), (1, 1), (0, 0))), 1
    )
    along_z = face_terms(
        jnp.pad(perm, ((0, 0), (0, 0), (1, 1))), jnp.pad(mask, ((0, 0), (0, 0), (1, 1))), 2
    )
    diagonal = (
        accum
        + along_x[1:]
        + along_x[:-1]
        + along_y[:, 1:]
        + along_y[:, :-1]
        + along_z[:, :, 1:]
        + along_z[:, :, :-1]
    )
    return (along_x, along_y, along_z, diagonal, accum)


def apply_flux(field, field_xpad, terms):
    along_x, along_y, along_z, diagonal, accum = terms
    flux = along_x[1:] * (field - field_xpad[:, 2:]) + along_x[:-1] * (field - field_xpad[:, :-2])
    ypad = jnp.pad(field, ((0, 0), (0, 0), (1, 1), (0, 0)))
    flux = (
        flux
        + along_y[:, 1:] * (field - ypad[:, :, 2:])
        + along_y[:, :-1] * (field - ypad[:, :, :-2])
    )
    zpad = jnp.pad(field, ((0, 0), (0, 0), (0, 0), (1, 1)))
    flux = (
        flux
        + along_z[:, :, 1:] * (field - zpad[:, :, :, 2:])
        + along_z[:, :, :-1] * (field - zpad[:, :, :, :-2])
    )
    return accum * field + flux


def inner_product(left, right):
    return jnp.einsum("axyz,bxyz->ab", left, right, precision=lax.Precision.HIGHEST)


def inverse_factor(gram):
    lower = jnp.linalg.cholesky(gram)
    eye_matrix = jnp.eye(gram.shape[0], dtype=gram.dtype)
    return lax.linalg.triangular_solve(lower, eye_matrix, left_side=True, lower=True)


def active_mask(x_index, ex_limit, ez_limit, ny_count, nz_count):
    inside_x = (x_index >= 0) & (x_index < ex_limit)
    inside_z = jnp.arange(nz_count, dtype=jnp.int32) < ez_limit
    joined = inside_x[:, None, None] & inside_z[None, None, :]
    return jnp.broadcast_to(joined, (x_index.shape[0], ny_count, nz_count)).astype(jnp.float32)


def selector(ez_limit, widths, nz_count, wmax):
    depth = jnp.arange(nz_count, dtype=jnp.int32)[None, :, None]
    layer = jnp.arange(wmax, dtype=jnp.int32)[None, None, :]
    wide = widths[:, None, None]
    return ((depth == ez_limit - wide + layer) & (layer < wide)).astype(jnp.float32)


def first_layers(field, wmax):
    count, nx_count, ny_count, nz_count = field.shape
    return field.reshape(count, nx_count * ny_count, nz_count)[:, :, :wmax].transpose(0, 2, 1)


def weighted_layers(field, perm, ez_limit, widths, wmax):
    count, nx_count, ny_count, nz_count = field.shape
    chosen = selector(ez_limit, widths, nz_count, wmax)
    scaled = (field * perm).reshape(count, nx_count * ny_count, nz_count)
    return jnp.einsum("apz,nzt->natp", scaled, chosen, precision=lax.Precision.HIGHEST)


def body(start_vectors, permeability, accumulation, extents, neighbour_ids, intersection_widths):
    width_x = permeability.shape[0]
    groups = lax.axis_size("inner")
    cells = groups * width_x * CY * CZ
    ex_limit = extents[0, 0]
    ez_limit = extents[0, 1]
    neighbours = neighbour_ids[0]
    widths = intersection_widths[0]
    x_index = lax.axis_index("inner") * width_x - 1 + jnp.arange(width_x + 2, dtype=jnp.int32)
    mask_xpad = active_mask(x_index, ex_limit, ez_limit, CY, CZ)
    perm_xpad = padded(permeability, (("inner", 0),), 1)
    terms = coefficients(perm_xpad, mask_xpad, accumulation)

    def image_of(field):
        field_xpad = padded(field, (("inner", 1),), 1)
        return (field, apply_flux(field, field_xpad, terms), terms[3])

    basis = start_vectors * mask_xpad[1:-1]
    center, image, diagonal = image_of(basis)
    basis = center - omega * image / diagonal
    center, image, diagonal = image_of(basis)
    smoothed = center - omega * image / diagonal
    gram = lax.psum(inner_product(smoothed, smoothed) / cells, "inner")
    basis = jnp.einsum(
        "ab,bxyz->axyz", inverse_factor(gram), smoothed, precision=lax.Precision.HIGHEST
    )
    basis, image, diagonal = image_of(basis)
    galerkin = lax.psum(inner_product(basis, image) / cells, "inner")
    own = weighted_layers(basis, permeability, ez_limit, widths, WMAX)
    piece = lax.all_gather(first_layers(basis, WMAX)[None], "subdomai", axis=0, tiled=True)
    count = piece.shape[0]
    hits = (neighbours[:, None] == jnp.arange(count, dtype=jnp.int32)[None, :]).astype(jnp.float32)
    partial_blocks = jnp.einsum("natp,sbtp->nsab", own, piece, precision=lax.Precision.HIGHEST)
    partial_sum = jnp.einsum("ns,nsab->nab", hits, partial_blocks, precision=lax.Precision.HIGHEST)
    coupling = lax.psum(partial_sum / cells, "inner")
    return (basis, galerkin[None], coupling[None])


def solution(mesh):
    return jax.shard_map(
        body,
        mesh=mesh,
        in_specs=(
            P(None, ("subdomai", "inner"), None, None),
            P(("subdomai", "inner"), None, None),
            P(("subdomai", "inner"), None, None),
            P("subdomai", None),
            P("subdomai", None),
            P("subdomai", None),
        ),
        out_specs=(
            P(None, ("subdomai", "inner"), None, None),
            P("subdomai", None, None),
            P("subdomai", None, None, None),
        ),
        check_vma=False,
    )
```

profile of v0, /device:TPU:2, one launch (start us, length us, event | category | flops | bytes accessed | tf_op | source)
XLA Modules:
  0.0 508.5 jit_solution(13701670428106044783)
XLA Ops:
  7.2 0.0 all-gather.3.cloned.1.call-start
  7.2 0.8 fusion.109
  8.0 1.3 collective-permute-start.1
  9.3 4.5 collective-permute-start
  13.8 1.3 fusion.110
  15.2 0.6 iota_compare_fusion.6
  15.8 0.7 compare_and_fusion
  16.5 0.1 and_convert_fusion
  16.6 5.7 %copy_multiply_fusion = f32[8,16,64,128]{3,0,2,1:T(8,128)S(1)} fusion(f32[8,16,64,128]{3,2,1,0:T(8,128)} %param.6, f32[16,128]{1,0:T(8,128)S(1)} %slice.226), kind=kLoop, calls=%fused_computation.66 | loop fusion | flops 1048576 | bytes 8396800 | tf_op jit(solution)/shard_map/mul | solution.py:129
  22.3 0.0 copy-start.3
  22.3 1.4 collective-permute-start.2
  23.8 4.6 collective-permute-start.3
  28.3 0.0 copy-done.8
  28.3 0.1 fusion.102
  28.5 0.6 fusion.83
  29.1 0.2 fusion.90
  29.3 0.0 collective-permute-done
  29.3 0.1 constant_dynamic-update-slice_fusion.3
  29.5 0.0 collective-permute-done.1
  29.5 0.1 add_divide_fusion
  29.6 0.4 fusion.108
  30.0 1.8 collective-permute-done.2
  31.8 1.2 collective-permute-done.3
  33.0 5.8 %fusion.7 = f32[8,16,64,128]{3,0,2,1:T(8,128)S(1)} fusion(f32[8,16,64,128]{3,0,2,1:T(8,128)S(1)} %copy_multiply_fusion, f32[8,1,64,128]{3,0,2,1:T(8,128)S(1)} %collective-permute-done.3, f32[8,1,64,128]{3,0,2,1:T(8,128)S(1)} %collective-permute-done.2, f32[16,64,128]{2,1,0:T(8,128)S(1)} %get-tuple-element.15, f32[16,64,128]{2,1,0:T(8,128)S(1)} %get-tuple-element.16, ...), kind=kLoop, calls=%fused_computation.13 | loop fusion | flops 25165824 | bytes 13107200 | tf_op jit(solution)/shard_map/sub | solution.py:131
  38.8 1.3 collective-permute-start.4
  40.1 5.2 %collective-permute-start.5 = (f32[8,1,64,128]{3,0,2,1:T(8,128)S(1)}, f32[8,1,64,128]{3,0,2,1:T(8,128)S(1)}, u32[]{:S(2)}, u32[]{:S(2)}) collective-permute-start(f32[8,1,64,128]{3,0,2,1:T(8,128)S(1)} %get-tuple-element.11), channel_id=1, source_target_pairs={{0,1},{1,2},{2,3},{3,4},{4,5},{5,6},{6,7},{7,8},{8,9},{9,10},{10,1... | collective-permute-start | bytes 786440 | tf_op jit(solution)/shard_map/ppermute | solution.py:21
  45.4 0.0 copy-done.9
  45.4 0.7 broadcast_subtract_fusion
  46.0 0.1 iota_add_fusion
  46.1 1.7 collective-permute-done.4
  47.8 1.3 collective-permute-done.5
  49.0 0.0 copy-done.4
  49.0 5.8 %fusion.17 = f32[8,16,64,128]{3,0,2,1:T(8,128)S(1)} fusion(f32[8,16,64,128]{3,0,2,1:T(8,128)S(1)} %fusion.7, f32[8,1,64,128]{3,0,2,1:T(8,128)S(1)} %collective-permute-done.5, f32[8,1,64,128]{3,0,2,1:T(8,128)S(1)} %collective-permute-done.4, f32[16,64,128]{2,1,0:T(8,128)S(1)} %get-tuple-element.15, f32[16,64,128]{2,1,0:T(8,128)S(1)} %get-tuple-element.16, ...), kind=kLoop, calls=%fused_computation.23 | loop fusion | flops 25165824 | bytes 13107200 | tf_op jit(solution)/shard_map/sub | solution.py:133
  54.8 0.0 copy-start
  54.8 2.0 copy-done
  56.8 9.0 %fusion.75 = f32[8,8]{0,1:T(8,128)S(1)} fusion(f32[8,16,64,128]{3,0,2,1:T(8,128)S(1)} %fusion.17), kind=kOutput, calls=%fused_computation.91 | convolution fusion | flops 100663360 | bytes 4194560 | tf_op jit(solution)/shard_map/axyz,bxyz->ab/dot_general | solution.py:77
  65.9 82.4 %psum.21 = f32[8,8]{0,1:T(8,128)S(1)} all-reduce(f32[8,8]{0,1:T(8,128)S(1)} %fusion.75), channel_id=1, replica_groups=mesh['subdomai'=8,'inner'=32] {'inner'}, use_global_device_ids=true, to_apply=%region_0.1 | all-reduce | flops 64 | bytes 512 | tf_op jit(solution)/shard_map/psum | solution.py:134
  148.2 0.1 copy.11
  148.3 0.7 cholesky.17
  149.1 0.6 compare_reduce_fusion
  149.7 0.6 fusion.99
  150.4 0.6 custom-call.6
  151.0 0.2 convolution_bitcast_fusion.1
  151.2 8.0 %broadcast_multiply_fusion = (f32[8,16,64,128]{3,0,2,1:T(8,128)}, f32[8,16,64,128]{3,0,2,1:T(8,128)S(1)}) fusion(f32[16,64,128]{2,1,0:T(8,128)S(1)} %copy-done.2, f32[8,8,1,1]{1,0,3,2:T(8,128)S(1)} %convolution_bitcast_fusion.1, f32[8,16,64,128]{3,0,2,1:T(8,128)} %copy-done), kind=kOutput, calls=%fused_computation.75 | convolution fusion | flops 101711872 | bytes 13107456 | tf_op jit(solution)/shard_map/ab,bxyz->axyz/dot_general | solution.py:135
  159.2 2.0 copy-done.1
  161.1 2.3 slice_bitcast_fusion
  163.5 0.0 all-gather.3.cloned.1.call-update
  163.5 0.1 iota_compare_fusion.1
  163.6 5.2 %copy.15 = f32[8,16,64,128]{3,2,1,0:T(8,128)} copy(f32[8,16,64,128]{3,0,2,1:T(8,128)} %copy-done.1) | data formatting | bytes 8388608
  168.8 1.1 fusion.105
  169.9 1.3 collective-permute-start.6
  171.2 5.3 %collective-permute-start.7 = (f32[8,1,64,128]{3,0,2,1:T(8,128)S(1)}, f32[8,1,64,128]{3,0,2,1:T(8,128)}, u32[]{:S(2)}, u32[]{:S(2)}) collective-permute-start(f32[8,1,64,128]{3,0,2,1:T(8,128)S(1)} %get-tuple-element.9), channel_id=1, source_target_pairs={{0,1},{1,2},{2,3},{3,4},{4,5},{5,6},{6,7},{7,8},{8,9},{9,10},{10,1... | collective-permute-start | bytes 786440 | tf_op jit(solution)/shard_map/ppermute | solution.py:21
  176.4 11.0 %fusion.55 = f32[6,4,8,1024]{3,1,2,0:T(4,128)} fusion(f32[8,1024,128,1]{2,0,1,3:T(8,128)S(1)} %bitcast.66, s32[6,4]{1,0:T(8,128)S(1)} %iota_add_fusion, pred[6,4]{1,0:T(8,128)(4,1)S(1)} %iota_compare_fusion.1), kind=kOutput, calls=%fused_computation.64 | convolution fusion | flops 301996032 | bytes 4980856 | tf_op jit(solution)/shard_map/apz,nzt->natp/dot_general | solution.py:109
  187.5 0.0 collective-permute-done.6
  187.5 0.0 collective-permute-done.7
  187.5 0.0 copy-done.5
  187.5 19.8 %fusion.76 = f32[8,8]{0,1:T(8,128)S(1)} fusion(f32[8,16,64,128]{3,0,2,1:T(8,128)} %copy-done.1, f32[8,1,64,128]{3,0,2,1:T(8,128)} %collective-permute-done.7, f32[8,1,64,128]{3,0,2,1:T(8,128)S(1)} %collective-permute-done.6, f32[16,64,128]{2,1,0:T(8,128)S(1)} %get-tuple-element.16, f32[16,64,128]{2,1,0:T(8,128)S(1)} %get-tuple-element.14, ...), kind=kOutput, calls=%fused_computation.92 | convolution fusion | flops 122683456 | bytes 12583168 | tf_op jit(solution)/shard_map/axyz,bxyz->ab/dot_general | solution.py:77
  207.3 0.1 copy.14
  207.4 123.8 %all-gather.3.cloned.1.call-done = f32[64,4,1024]{1,0,2:T(8,128)} async-done(((f32[8,4,1024]{1,0,2:T(8,128)}), f32[64,4,1024]{1,0,2:T(8,128)}) %all-gather.3.cloned.1.call-update) | async-done | bytes 1048592 | tf_op jit(solution)/shard_map/all_gather | solution.py:141
  331.2 19.6 %copy.22 = f32[8,8,4,1024,1]{3,1,2,4,0:T(8,128)S(1)} copy(f32[8,8,4,1024,1]{2,1,0,3,4:T(8,128)} %bitcast.65) | data formatting | bytes 2097152 | tf_op jit(solution)/shard_map/all_gather | solution.py:141
  350.9 6.9 %convolution_bitcast_fusion = f32[6,8,8,8]{2,3,0,1:T(8,128)S(1)} fusion(f32[8,8,4,1024,1]{3,1,2,4,0:T(8,128)S(1)} %copy.22, f32[6,4,8,1024]{3,1,2,0:T(4,128)S(1)} %copy-done.10), kind=kOutput, calls=%fused_computation.87 | convolution fusion | flops 150994944 | bytes 1847296 | tf_op jit(solution)/shard_map/natp,sbtp->nsab/dot_general | solution.py:144
  357.8 0.1 copy.25
  357.9 0.2 fusion.97
  358.1 143.5 %all-reduce.10 = (f32[1,8,8]{2,1,0:T(8,128)}, f32[1,6,8,8]{3,2,1,0:T(8,128)}) all-reduce(f32[1,8,8]{2,1,0:T(8,128)S(1)} %bitcast.68, f32[1,6,8,8]{3,2,1,0:T(8,128)S(1)} %multiply_bitcast_fusion), channel_id=1, replica_groups=mesh['subdomai'=8,'inner'=32] {'inner'}, use_global_device_ids=true, to_apply=%region_3.4 | all-reduce | flops 448 | bytes 3584 | tf_op jit(solution)/shard_map/psum | solution.py:139
  (24 shorter events, 0.2 us)
Async XLA Ops:
  7.2 324.1 %all-gather.3.cloned.1.call-start = ((), (), s32[]{:S(2)}) async-start(), calls=%async_computation | async-start | bytes 37748736 | tf_op jit(solution)/shard_map/all_gather | solution.py:141
  8.0 21.5 %collective-permute-start.1 = (f32[1,64,128]{2,1,0:T(8,128)S(1)}, f32[1,64,128]{2,1,0:T(8,128)S(1)}, u32[]{:S(2)}, u32[]{:S(2)}) collective-permute-start(f32[1,64,128]{2,1,0:T(8,128)S(1)} %get-tuple-element.21), channel_id=1, source_target_pairs={{1,0},{2,1},{3,2},{4,3},{5,4},{6,5},{7,6},{8,7},{9,8},{10,9},{11,1... | collective-permute-start | bytes 98312 | tf_op jit(solution)/shard_map/ppermute | solution.py:22
  9.3 20.0 %collective-permute-start = (f32[1,64,128]{2,1,0:T(8,128)S(1)}, f32[1,64,128]{2,1,0:T(8,128)S(1)}, u32[]{:S(2)}, u32[]{:S(2)}) collective-permute-start(f32[1,64,128]{2,1,0:T(8,128)S(1)} %get-tuple-element.22), channel_id=1, source_target_pairs={{0,1},{1,2},{2,3},{3,4},{4,5},{5,6},{6,7},{7,8},{8,9},{9,10},{10,1... | collective-permute-start | bytes 98312 | tf_op jit(solution)/shard_map/ppermute | solution.py:21
  16.6 11.8 %copy-start.8 = (s32[1,6]{1,0:T(1,128)S(1)}, s32[1,6]{1,0:T(1,128)}, u32[]{:S(2)}) copy-start(s32[1,6]{1,0:T(1,128)} %param.10) | copy-start | bytes 76
  16.6 11.9 %copy-start.2 = (f32[16,64,128]{2,1,0:T(8,128)S(1)}, f32[16,64,128]{2,1,0:T(8,128)}, u32[]{:S(2)}) copy-start(f32[16,64,128]{2,1,0:T(8,128)} %param.7) | copy-start | bytes 1572868
  22.3 7.3 %copy-start.3 = (f32[16,64,128]{2,1,0:T(8,128)S(1)}, f32[16,64,128]{2,1,0:T(8,128)}, u32[]{:S(2)}) copy-start(f32[16,64,128]{2,1,0:T(8,128)} %param.8) | copy-start | bytes 1572868
  22.3 9.5 %collective-permute-start.2 = (f32[8,1,64,128]{3,0,2,1:T(8,128)S(1)}, f32[8,1,64,128]{3,0,2,1:T(8,128)S(1)}, u32[]{:S(2)}, u32[]{:S(2)}) collective-permute-start(f32[8,1,64,128]{3,0,2,1:T(8,128)S(1)} %get-tuple-element.12), channel_id=1, source_target_pairs={{1,0},{2,1},{3,2},{4,3},{5,4},{6,5},{7,6},{8,7},{9,8},{10,9},{11,1... | collective-permute-start | bytes 786440 | tf_op jit(solution)/shard_map/ppermute | solution.py:22
  23.8 9.3 %collective-permute-start.3 = (f32[8,1,64,128]{3,0,2,1:T(8,128)S(1)}, f32[8,1,64,128]{3,0,2,1:T(8,128)S(1)}, u32[]{:S(2)}, u32[]{:S(2)}) collective-permute-start(f32[8,1,64,128]{3,0,2,1:T(8,128)S(1)} %get-tuple-element.13), channel_id=1, source_target_pairs={{0,1},{1,2},{2,3},{3,4},{4,5},{5,6},{6,7},{7,8},{8,9},{9,10},{10,1... | collective-permute-start | bytes 786440 | tf_op jit(solution)/shard_map/ppermute | solution.py:21
  30.0 19.0 %copy-start.4 = (f32[16,64,128]{2,1,0:T(8,128)}, f32[16,64,128]{2,1,0:T(8,128)S(1)}, u32[]{:S(2)}) copy-start(f32[16,64,128]{2,1,0:T(8,128)S(1)} %get-tuple-element.19) | copy-start | bytes 1572868
  30.0 19.0 %copy-start.6 = (f32[16,64,128]{2,1,0:T(8,128)}, f32[16,64,128]{2,1,0:T(8,128)S(1)}, u32[]{:S(2)}) copy-start(f32[16,64,128]{2,1,0:T(8,128)S(1)} %get-tuple-element.20) | copy-start | bytes 1572868
  33.0 12.3 %copy-start.9 = (s32[1,6]{1,0:T(1,128)S(1)}, s32[1,6]{1,0:T(1,128)}, u32[]{:S(2)}) copy-start(s32[1,6]{1,0:T(1,128)} %param.11) | copy-start | bytes 76
  38.8 8.9 %collective-permute-start.4 = (f32[8,1,64,128]{3,0,2,1:T(8,128)S(1)}, f32[8,1,64,128]{3,0,2,1:T(8,128)S(1)}, u32[]{:S(2)}, u32[]{:S(2)}) collective-permute-start(f32[8,1,64,128]{3,0,2,1:T(8,128)S(1)} %get-tuple-element.10), channel_id=1, source_target_pairs={{1,0},{2,1},{3,2},{4,3},{5,4},{6,5},{7,6},{8,7},{9,8},{10,9},{11,1... | collective-permute-start | bytes 786440 | tf_op jit(solution)/shard_map/ppermute | solution.py:22
  40.1 8.9 %collective-permute-start.5 = (f32[8,1,64,128]{3,0,2,1:T(8,128)S(1)}, f32[8,1,64,128]{3,0,2,1:T(8,128)S(1)}, u32[]{:S(2)}, u32[]{:S(2)}) collective-permute-start(f32[8,1,64,128]{3,0,2,1:T(8,128)S(1)} %get-tuple-element.11), channel_id=1, source_target_pairs={{0,1},{1,2},{2,3},{3,4},{4,5},{5,6},{6,7},{7,8},{8,9},{9,10},{10,1... | collective-permute-start | bytes 786440 | tf_op jit(solution)/shard_map/ppermute | solution.py:21
  54.8 2.0 copy-start
  159.2 2.0 copy-start.1
  163.6 12.9 %copy-start.7 = (f32[8,16,64,128]{3,0,2,1:T(8,128)S(1)}, f32[8,16,64,128]{3,0,2,1:T(8,128)}, u32[]{:S(2)}) copy-start(f32[8,16,64,128]{3,0,2,1:T(8,128)} %get-tuple-element.27) | copy-start | bytes 12582916
  168.8 18.7 %copy-start.5 = (f32[16,64,128]{2,1,0:T(8,128)S(1)}, f32[16,64,128]{2,1,0:T(8,128)}, u32[]{:S(2)}) copy-start(f32[16,64,128]{2,1,0:T(8,128)} %copy-done.4) | copy-start | bytes 1572868
  169.9 17.6 %collective-permute-start.6 = (f32[8,1,64,128]{3,0,2,1:T(8,128)S(1)}, f32[8,1,64,128]{3,0,2,1:T(8,128)S(1)}, u32[]{:S(2)}, u32[]{:S(2)}) collective-permute-start(f32[8,1,64,128]{3,0,2,1:T(8,128)S(1)} %get-tuple-element.8), channel_id=1, source_target_pairs={{1,0},{2,1},{3,2},{4,3},{5,4},{6,5},{7,6},{8,7},{9,8},{10,9},{11,1... | collective-permute-start | bytes 786440 | tf_op jit(solution)/shard_map/ppermute | solution.py:22
  171.2 16.3 %collective-permute-start.7 = (f32[8,1,64,128]{3,0,2,1:T(8,128)S(1)}, f32[8,1,64,128]{3,0,2,1:T(8,128)}, u32[]{:S(2)}, u32[]{:S(2)}) collective-permute-start(f32[8,1,64,128]{3,0,2,1:T(8,128)S(1)} %get-tuple-element.9), channel_id=1, source_target_pairs={{0,1},{1,2},{2,3},{3,4},{4,5},{5,6},{6,7},{7,8},{8,9},{9,10},{10,1... | collective-permute-start | bytes 786440 | tf_op jit(solution)/shard_map/ppermute | solution.py:21
  331.2 19.7 %copy-start.10 = (f32[6,4,8,1024]{3,1,2,0:T(4,128)S(1)}, f32[6,4,8,1024]{3,1,2,0:T(4,128)}, u32[]{:S(2)}) copy-start(f32[6,4,8,1024]{3,1,2,0:T(4,128)} %fusion.55) | copy-start | bytes 2359300
Sparse Core Ops, SparseCore 0:
  163.6 167.5 all-gather.2
where the time goes:
time: 509 us; the launch traced here: 508 us
  blocking collectives  226 us (44%)
  waiting for transfers between devices  130 us (26%)
  matrix products  55.1 us (11%)
  local copies, waits for them, and re-layouts  34.9 us (7%)
  starting transfers between devices  24.9 us (5%)
  other arithmetic  23.5 us (5%)
  between operations  14.4 us (3%)
    psum x1, blocking collectives, body(): galerkin = lax.psum(inner_product(basis, image) / cells, 'inner')  143 us
    all_gather x1, waiting for transfers between devices, body(): lax.all_gather(first_layers(basis, WMAX)[None], 'subdomai', axis=0, tiled...  124 us
    psum x1, blocking collectives, body(): gram = lax.psum(inner_product(smoothed, smoothed) / cells, 'inner')  82.4 us
    dot_general x2, matrix products, inner_product(): jnp.einsum('axyz,bxyz->ab', left, right, precision=lax.Precision.HIGHEST)  28.8 us
    all_gather x1, local copies, waits for them, and re-layouts, body(): lax.all_gather(first_layers(basis, WMAX)[None], 'subdomai', axis=0, tiled...  19.6 us
    ppermute x4, starting transfers between devices, padded(): before = lax.ppermute(last, axis, up)  19.6 us
    dot_general x1, matrix products, weighted_layers(): jnp.einsum('apz,nzt->natp', scaled, chosen, precision=lax.Precision.HIGHEST)  11 us
  transfers between devices with their start and end apart: 9, of which 5 were waited for; matrix products, arithmetic and copies ran while one was open for 9% of the time, Pallas kernels for 0%

commit v1 on v0

v1 whole, which is shorter than its diff:
```python
import functools
import jax
import jax.numpy as jnp
from jax import lax
from jax.experimental import pallas as pl
from jax.experimental.pallas import tpu as pltpu
from jax.sharding import PartitionSpec as P

F32 = jnp.float32
K = 8
NB = 6
WMAX = 4
CY = 64
CZ = 128
OMEGA = 0.6
SLAB = 16 * CY
HALO = 160
HALO_ACC = 96
OFF = HALO + 8
RT = SLAB + 2 * OFF
PACK = K * HALO + HALO + HALO_ACC
PAIRS = [(a, b) for b in range(K) for a in range(b + 1)]
NP = len(PAIRS)
HIGHEST = lax.Precision.HIGHEST
VMEM = pl.BlockSpec(memory_space=pltpu.VMEM)
SMEM = pl.BlockSpec(memory_space=pltpu.SMEM)
ANY = pl.BlockSpec(memory_space=pl.ANY)


def shape(*dims):
    return jax.ShapeDtypeStruct(dims, F32)


def rows_loop(lo, hi, step, init=(), tiles=4):
    def one(i, carry):
        stores = []
        for j in range(tiles):
            more, carry = step(pl.multiple_of(lo + OFF + (i * tiles + j) * 8, 8), carry)
            stores += more
        for ref, place, value in stores:
            ref[place] = value
        return carry

    assert (hi - lo) % (8 * tiles) == 0
    return lax.fori_loop(0, (hi - lo) // (8 * tiles), one, init)


def tile_at(row):
    return (pl.ds(row, 8), slice(None))


def field_at(a, row):
    return (a, pl.ds(row, 8), slice(None))


def lanes():
    return lax.broadcasted_iota(jnp.int32, (8, CZ), 1)


def sublanes():
    return lax.broadcasted_iota(jnp.int32, (8, CZ), 0)


def at(ref, row):
    return ref[pl.ds(row, 8), :]


def fat(ref, a, row):
    return ref[a, pl.ds(row, 8), :]


def layer_of(row):
    return lax.shift_right_arithmetic(row + (192 - OFF), 6) - 3


def active(scal, row, more=0):
    x = scal[2] + layer_of(row) + more
    return jnp.where((x >= 0) & (x < scal[0]), 1.0, 0.0).astype(F32)


def faces(scal, kp, fx, fy, fz, lo, hi):
    mz = jnp.where(lanes() < scal[1], 2.0, 0.0).astype(F32)
    mzz = jnp.where(lanes() < scal[1] - 1, 2.0, 0.0).astype(F32)
    sub = sublanes()

    def step(r, carry):
        here = active(scal, r)
        there = active(scal, r, 1)
        k = at(kp, r)
        kx = at(kp, r + CY)
        ky = at(kp, r + 1)
        kz = pltpu.roll(k, CZ - 1, 1)
        inside = jnp.where(((r + (192 - OFF)) & (CY - 1)) == CY - 8, 0.0, 1.0).astype(F32)
        my = jnp.where(sub == 7, inside, 1.0)
        stores = [
            (fx, tile_at(r), (mz * (here * there)) * k * kx / (k + kx)),
            (fy, tile_at(r), (mz * here) * my * k * ky / (k + ky)),
            (fz, tile_at(r), (mzz * here) * k * kz / (k + kz)),
        ]
        return stores, carry

    rows_loop(lo, hi, step)


def weights(ac, fx, fy, fz, w, lo, hi):
    def step(r, carry):
        z = at(fz, r)
        diagonal = (
            (at(ac, r) + at(fx, r))
            + (at(fx, r - CY) + at(fy, r))
            + (at(fy, r - 1) + z)
            + pltpu.roll(z, 1, 1)
        )
        return [(w, tile_at(r), OMEGA / diagonal)], carry

    rows_loop(lo, hi, step)


def smooth(scal, src, dst, fx, fy, fz, w, lo, hi, masked):
    mz = jnp.where(lanes() < scal[1], 1.0 - OMEGA, 0.0).astype(F32)

    def step(r, carry):
        wt = at(w, r)
        z = at(fz, r)
        xp = wt * at(fx, r)
        xm = wt * at(fx, r - CY)
        yp = wt * at(fy, r)
        ym = wt * at(fy, r - 1)
        zp = wt * z
        zm = wt * pltpu.roll(z, 1, 1)
        centre = mz * active(scal, r) if masked else 1.0 - OMEGA
        stores = []
        for a in range(K):
            v = fat(src, a, r)
            new = (
                (centre * v + xp * fat(src, a, r + CY))
                + (xm * fat(src, a, r - CY) + yp * fat(src, a, r + 1))
                + (ym * fat(src, a, r - 1) + zp * pltpu.roll(v, CZ - 1, 1))
                + zm * pltpu.roll(v, 1, 1)
            )
            stores.append((dst, field_at(a, r), new))
        return stores, carry

    rows_loop(lo, hi, step)


def gram_sums(s, lo, hi, acc):
    def step(r, acc):
        v = [fat(s, a, r) for a in range(K)]
        return [], tuple(t + v[a] * v[b] for t, (a, b) in zip(acc, PAIRS))

    return rows_loop(lo, hi, step, tuple(acc), tiles=2)


def flux_sums(s, ac, fx, fy, fz, lo, hi, acc, before=True, after=True):
    def step(r, acc):
        out = list(acc)
        z = at(fz, r)
        xp = at(fx, r)
        xm = at(fx, r - CY)
        yp = at(fy, r)
        ym = at(fy, r - 1)
        d = at(ac, r)
        v = [fat(s, a, r) for a in range(K)]
        g = [c - pltpu.roll(c, CZ - 1, 1) for c in v]
        for b in range(K):
            c = v[b]
            image = d * c + yp * (c - fat(s, b, r + 1)) + ym * (c - fat(s, b, r - 1))
            if after:
                image = image + xp * (c - fat(s, b, r + CY))
            if before:
                image = image + xm * (c - fat(s, b, r - CY))
            slope = z * g[b]
            for a in range(b + 1):
                p = b * (b + 1) // 2 + a
                out[p] = out[p] + (v[a] * image + g[a] * slope)
        return [], tuple(out)

    return rows_loop(lo, hi, step, tuple(acc), tiles=1)


def crossing_sums(s, fx, lo, hi, acc):
    def step(r, acc):
        f = at(fx, r)
        d = [fat(s, a, r) - fat(s, a, r + CY) for a in range(K)]
        e = [f * t for t in d]
        return [], tuple(t + d[a] * e[b] for t, (a, b) in zip(acc, PAIRS))

    return rows_loop(lo, hi, step, tuple(acc), tiles=1)


def turned(scal, s, kp, first, window, tile, ptile, blocks):
    start = scal[1] - WMAX

    def step(block, row, lane):
        ptile[...] = kp[pl.ds(row, CZ), :].T
        kw = ptile[pl.ds(start, WMAX), :]
        for a in range(K):
            tile[a] = s[a, pl.ds(row, CZ), :].T
        for a in range(K):
            u = tile[a, pl.ds(start, WMAX), :] * kw
            f = tile[a, pl.ds(0, WMAX), :]
            for t in range(WMAX):
                first[pl.ds(t * K + a, 1), pl.ds(lane, CZ)] = f[t : t + 1]
                window[pl.ds(t * K + a, 1), pl.ds(lane, CZ)] = u[t : t + 1]

    def one(block, carry):
        step(block, pl.multiple_of(OFF + block * CZ, 8), pl.multiple_of((block - blocks[0]) * CZ, CZ))
        return carry

    lax.fori_loop(blocks[0], blocks[1], one, 0)


def copy_all(pairs, sem):
    copies = [pltpu.make_async_copy(src, dst, sem.at[i]) for i, (src, dst) in enumerate(pairs)]
    for c in copies:
        c.start()
    return copies


def wait_all(copies):
    for c in copies:
        c.wait()


def pack_kernel(sv, perm, acc, down, up, sem):
    pairs = []
    for out, lo, acc_lo in ((down, 0, 0), (up, SLAB - HALO, SLAB - HALO_ACC)):
        for a in range(K):
            pairs.append((sv.at[a, pl.ds(lo, HALO)], out.at[pl.ds(a * HALO, HALO)]))
        pairs.append((perm.at[pl.ds(lo, HALO)], out.at[pl.ds(K * HALO, HALO)]))
        pairs.append((acc.at[pl.ds(acc_lo, HALO_ACC)], out.at[pl.ds((K + 1) * HALO, HALO_ACC)]))
    wait_all(copy_all(pairs, sem))


INSIDE = SLAB - 4 * CY


def interior_kernel(
    scal, sv, perm, acc, si, ve, gram, flux, first, window, v0, v1, s, kp, ac, fx, fy, fz, w, tile, ptile, sem
):
    slab = pl.ds(OFF, SLAB)
    a, b, c = copy_all([(perm, kp.at[slab]), (acc, ac.at[slab]), (sv, v0.at[:, slab])], sem)
    a.wait()
    faces(scal, kp, fx, fy, fz, 0, SLAB - CY)
    b.wait()
    weights(ac, fx, fy, fz, w, CY, SLAB - CY)
    c.wait()
    smooth(scal, v0, v1, fx, fy, fz, w, CY, SLAB - CY, True)
    smooth(scal, v1, s, fx, fy, fz, w, 2 * CY, SLAB - 2 * CY, False)
    out = copy_all(
        [
            (s.at[:, pl.ds(OFF + 2 * CY, INSIDE)], si),
            (v1.at[:, pl.ds(OFF + CY, CZ)], ve.at[0]),
            (v1.at[:, pl.ds(OFF + SLAB - CY - CZ, CZ)], ve.at[1]),
        ],
        sem,
    )
    zero = [jnp.zeros((8, CZ), F32)] * NP
    for i, t in enumerate(gram_sums(s, 2 * CY, SLAB - 2 * CY, zero)):
        gram[i] = t
    for i, t in enumerate(flux_sums(s, ac, fx, fy, fz, 3 * CY, SLAB - 3 * CY, zero)):
        flux[i] = t
    turned(scal, s, kp, first, window, tile, ptile, (1, 7))
    wait_all(out)


def edge_kernel(
    scal, left, right, sv, perm, acc, si, ve, gram, flux, firsti, windowi,
    se, first, window, part, v0, v1, s, kp, ac, fx, fy, fz, w, fe, we, tile, ptile, sem,
):
    pairs = []
    far = SLAB - 2 * CZ
    for src, lo, acc_lo, near in ((left, -HALO, -HALO_ACC, 0), (right, SLAB, SLAB, far)):
        pairs.append((src.at[pl.ds(K * HALO, HALO)], kp.at[pl.ds(OFF + lo, HALO)]))
        pairs.append((src.at[pl.ds((K + 1) * HALO, HALO_ACC)], ac.at[pl.ds(OFF + acc_lo, HALO_ACC)]))
        for a in range(K):
            pairs.append((src.at[pl.ds(a * HALO, HALO)], v0.at[a, pl.ds(OFF + lo, HALO)]))
        pairs.append((perm.at[pl.ds(near, 2 * CZ)], kp.at[pl.ds(OFF + near, 2 * CZ)]))
        pairs.append((acc.at[pl.ds(near, 2 * CZ)], ac.at[pl.ds(OFF + near, 2 * CZ)]))
        pairs.append((sv.at[:, pl.ds(near, 2 * CZ)], v0.at[:, pl.ds(OFF + near, 2 * CZ)]))
    pairs.append((ve.at[0], v1.at[:, pl.ds(OFF + CY, CZ)]))
    pairs.append((ve.at[1], v1.at[:, pl.ds(OFF + SLAB - CY - CZ, CZ)]))
    pairs.append((si.at[:, pl.ds(0, CZ)], s.at[:, pl.ds(OFF + CZ, CZ)]))
    pairs.append((si.at[:, pl.ds(INSIDE - CZ, CZ)], s.at[:, pl.ds(OFF + SLAB - 2 * CZ, CZ)]))
    wait_all(copy_all(pairs, sem))
    faces(scal, kp, fx, fy, fz, -HALO, 3 * CY)
    faces(scal, kp, fx, fy, fz, SLAB - 4 * CY, SLAB + HALO_ACC)
    weights(ac, fx, fy, fz, w, -HALO_ACC, 2 * CY)
    weights(ac, fx, fy, fz, w, SLAB - 2 * CY, SLAB + HALO_ACC)
    smooth(scal, v0, v1, fx, fy, fz, w, -HALO_ACC, CY, True)
    smooth(scal, v0, v1, fx, fy, fz, w, SLAB - CY, SLAB + HALO_ACC, True)
    smooth(scal, v1, s, fx, fy, fz, w, -32, 2 * CY, False)
    smooth(scal, v1, s, fx, fy, fz, w, SLAB - 2 * CY, SLAB + 32, False)
    out = copy_all(
        [
            (s.at[:, pl.ds(OFF, CZ)], se.at[0]),
            (s.at[:, pl.ds(OFF + SLAB - CZ, CZ)], se.at[1]),
        ],
        sem,
    )
    for whole, inside in ((first, firsti), (window, windowi)):
        whole[:, pl.ds(CZ, INSIDE)] = inside[...]
    for i, lane in ((0, 0), (7, SLAB - CZ)):
        turned(scal, s, kp, fe, we, tile, ptile, (i, i + 1))
        first[:, pl.ds(lane, CZ)] = fe[...]
        window[:, pl.ds(lane, CZ)] = we[...]
    acc = [gram[i] for i in range(NP)]
    acc = gram_sums(s, 0, 2 * CY, acc)
    acc = gram_sums(s, SLAB - 2 * CY, SLAB, acc)
    row, lane = sublanes(), lanes()
    res = jnp.zeros((8, CZ), F32)
    for b, col in enumerate(lane_sums(acc)):
        res = jnp.where(lane == NB * K + b, col, res)
    acc = [flux[i] for i in range(NP)]
    acc = flux_sums(s, ac, fx, fy, fz, 0, CY, acc, before=False)
    acc = flux_sums(s, ac, fx, fy, fz, CY, 3 * CY, acc)
    acc = flux_sums(s, ac, fx, fy, fz, SLAB - 3 * CY, SLAB - CY, acc)
    acc = flux_sums(s, ac, fx, fy, fz, SLAB - CY, SLAB, acc, after=False)
    acc = crossing_sums(s, fx, -32, 0, acc)
    acc = crossing_sums(s, fx, SLAB - CY, SLAB - 32, acc)
    for b, col in enumerate(lane_sums(acc)):
        res = jnp.where(lane == NB * K + K + b, col, res)
    part[...] = res
    wait_all(out)


def lane_sums(acc):
    row = sublanes()
    cols = []
    for b in range(K):
        x = jnp.zeros((8, CZ), F32)
        for a in range(K):
            p = PAIRS.index((min(a, b), max(a, b)))
            x = jnp.where(row == a, jnp.sum(acc[p], axis=0, keepdims=True), x)
        cols.append(jnp.sum(x, axis=1, keepdims=True))
    return cols


def couple_kernel(scal, window, near, far, part, msg, chosen, prod):
    for n in range(NB):
        m = scal[8 + n] ^ scal[3]
        place = lax.shift_right_logical(m, 1)
        odd = (m & 1) == 1
        for t in range(WMAX):
            rows = pl.ds(t * K, K)
            chosen[pl.ds((t * NB + n) * K, K), :] = jnp.where(odd, far[place, rows, :], near[place, rows, :])
    prod[:, : WMAX * NB * K] = lax.dot_general(
        window[...], chosen[...], (((1,), (1,)), ((), ())), precision=HIGHEST, preferred_element_type=F32
    )
    lane = lax.broadcasted_iota(jnp.int32, (8, 2 * CZ), 1)
    total = jnp.zeros((8, 2 * CZ), F32)
    for t in range(WMAX):
        x = jnp.zeros((8, 2 * CZ), F32)
        for n in range(NB):
            width = scal[16 + n]
            d = jnp.where(t < width, WMAX - width + t, 0)
            v = prod[pl.ds(pl.multiple_of(d * K, K), K), :]
            lo = (t * NB + n) * K
            keep = (lane >= lo) & (lane < lo + K) & (t < width)
            x = jnp.where(keep, v, x)
        total = total + (pltpu.roll(x, 2 * CZ - t * NB * K, 1) if t else x)
    res = part[...] + total[:, :CZ]
    for i in range(msg.shape[0]):
        msg[i] = res


def factor_kernel(scale, got, total, inverse, spread, galerkin):
    m = jnp.sum(got[...], axis=0) * scale
    total[...] = m
    row, lane = sublanes(), lanes()
    e = jnp.where(lane < K, pltpu.roll(m, CZ - NB * K, 1), jnp.where(lane == row + K, 1.0, 0.0))
    e = jnp.where(lane < 2 * K, e, 0.0)
    root = jnp.ones((8, 1), F32)
    for k in range(K):
        pivot = e[k : k + 1, k : k + 1]
        factor = jnp.where(row[:, :1] > k, e[:, k : k + 1] / pivot, 0.0)
        root = jnp.where(row[:, :1] == k, 1.0 / jnp.sqrt(pivot), root)
        e = e - factor * e[k : k + 1, :]
    li = jnp.where(lane < K, pltpu.roll(e * root, CZ - K, 1), 0.0)
    inverse[...] = li
    for i, (b, a) in enumerate(PAIRS):
        spread[i] = jnp.broadcast_to(li[a : a + 1, b : b + 1], (8, CZ))
    g = jnp.dot(li[:, :K], m[:, NB * K + K : NB * K + 2 * K], precision=HIGHEST, preferred_element_type=F32)
    galerkin[...] = lax.dot_general(
        g, li[:, :K], (((1,), (1,)), ((), ())), precision=HIGHEST, preferred_element_type=F32
    )


def change_kernel(si, se, spread, out):
    c = [spread[i] for i in range(NP)]
    edge = (pl.program_id(0) == 0) | (pl.program_id(0) == SLAB // CZ - 1)

    def rows(src):
        def step(i, carry):
            stores = []
            for j in range(2):
                r = pl.multiple_of(i * 16 + j * 8, 8)
                v = [src[a, pl.ds(r, 8), :] for a in range(K)]
                for a in range(K):
                    x = c[PAIRS.index((0, a))] * v[0]
                    for b in range(1, a + 1):
                        x = x + c[PAIRS.index((b, a))] * v[b]
                    stores.append((a, r, x))
            for a, r, x in stores:
                out[a, pl.ds(r, 8), :] = x
            return carry

        lax.fori_loop(0, CZ // 16, step, 0)

    @pl.when(edge)
    def _():
        rows(se.at[0])

    @pl.when(~edge)
    def _():
        rows(si)


def finish_kernel(scal, total, near, far, out):
    y = jnp.dot(near[0, :, :K], total[:, : NB * K], precision=HIGHEST, preferred_element_type=F32)
    for n in range(NB):
        m = scal[8 + n] ^ scal[3]
        place = lax.shift_right_logical(m, 1)
        li = jnp.where((m & 1) == 1, far[place], near[place])
        out[n] = lax.dot_general(
            y[:, n * K : n * K + K], li[:, :K], (((1,), (1,)), ((), ())), precision=HIGHEST,
            preferred_element_type=F32,
        )


def params(mib=40):
    return pltpu.CompilerParams(vmem_limit_bytes=mib * 1024 * 1024)


def cost(us):
    return pl.CostEstimate(flops=0, bytes_accessed=int(us * 3.0e6), transcendentals=0)


def swap(x, bits):
    return lax.ppermute(x, "subdomai", [(i, i ^ bits) for i in range(lax.axis_size("subdomai"))])


def gathered(x):
    near = jnp.stack([x, swap(x, 2), swap(x, 4), swap(x, 6)])
    return near, swap(near, 1)


def body(start_vectors, permeability, accumulation, extents, neighbour_ids, intersection_widths):
    groups = lax.axis_size("inner")
    cells = groups * SLAB * CZ
    inner = lax.axis_index("inner")
    own = lax.axis_index("subdomai")
    sv = start_vectors.reshape(K, SLAB, CZ)
    perm = permeability.reshape(SLAB, CZ)
    acc = accumulation.reshape(SLAB, CZ)
    scal = jnp.concatenate(
        [
            extents[0],
            jnp.stack([inner * 16, own]).astype(jnp.int32),
            jnp.zeros(4, jnp.int32),
            neighbour_ids[0],
            jnp.zeros(2, jnp.int32),
            intersection_widths[0],
            jnp.zeros(10, jnp.int32),
        ]
    )
    down, up = pl.pallas_call(
        pack_kernel,
        out_shape=(shape(PACK, CZ),) * 2,
        in_specs=[ANY] * 3,
        out_specs=(VMEM,) * 2,
        scratch_shapes=[pltpu.SemaphoreType.DMA((20,))],
        name="pack",
    )(sv, perm, acc)
    right = lax.ppermute(down, "inner", [(i, (i - 1) % groups) for i in range(groups)])
    left = lax.ppermute(up, "inner", [(i, (i + 1) % groups) for i in range(groups)])
    field, plain = pltpu.VMEM((K, RT, CZ), F32), pltpu.VMEM((RT, CZ), F32)
    scratch = [field] * 3 + [plain] * 6
    turning = [pltpu.VMEM((K, CZ, CZ), F32), pltpu.VMEM((CZ, CZ), F32)]
    si, ve, gram, flux, first, window = pl.pallas_call(
        interior_kernel,
        out_shape=(shape(K, INSIDE, CZ), shape(2, K, CZ, CZ))
        + (shape(NP, 8, CZ),) * 2
        + (shape(WMAX * K, INSIDE),) * 2,
        in_specs=[SMEM, ANY, ANY, ANY],
        out_specs=(ANY,) * 2 + (VMEM,) * 4,
        scratch_shapes=scratch + turning + [pltpu.SemaphoreType.DMA((3,))],
        compiler_params=params(),
        cost_estimate=cost(10),
        name="interior",
    )(scal, sv, perm, acc)
    se, first, window, part = pl.pallas_call(
        edge_kernel,
        out_shape=(shape(2, K, CZ, CZ),) + (shape(WMAX * K, SLAB),) * 2 + (shape(8, CZ),),
        in_specs=[SMEM] + [ANY] * 7 + [VMEM] * 4,
        out_specs=(ANY,) + (VMEM,) * 3,
        scratch_shapes=scratch
        + [pltpu.VMEM((WMAX * K, CZ), F32)] * 2
        + turning
        + [pltpu.SemaphoreType.DMA((30,))],
        compiler_params=params(),
        cost_estimate=cost(3),
        name="edge",
    )(scal, left, right, sv, perm, acc, si, ve, gram, flux, first, window)
    near, far = gathered(first)
    msg = pl.pallas_call(
        couple_kernel,
        out_shape=shape(groups, 8, CZ),
        in_specs=[SMEM] + [VMEM] * 4,
        out_specs=VMEM,
        scratch_shapes=[pltpu.VMEM((WMAX * NB * K, SLAB), F32), pltpu.VMEM((WMAX * K, 2 * CZ), F32)],
        compiler_params=params(),
        cost_estimate=cost(1),
        name="couple",
    )(scal, window, near, far, part)
    got = lax.all_to_all(msg, "inner", 0, 0)
    total, inverse, spread, galerkin = pl.pallas_call(
        functools.partial(factor_kernel, 1.0 / cells),
        out_shape=(shape(8, CZ), shape(8, CZ), shape(NP, 8, CZ), shape(K, K)),
        in_specs=[VMEM],
        out_specs=(VMEM,) * 4,
        compiler_params=params(),
        cost_estimate=cost(1),
        name="factor",
    )(got)
    lnear, lfar = gathered(inverse)
    basis = pl.pallas_call(
        change_kernel,
        out_shape=shape(K, SLAB, CZ),
        grid=(SLAB // CZ,),
        in_specs=[
            pl.BlockSpec((K, CZ, CZ), lambda i: (0, jnp.clip(i - 1, 0, INSIDE // CZ - 1), 0)),
            pl.BlockSpec((1, K, CZ, CZ), lambda i: (jnp.where(i > 0, 1, 0), 0, 0, 0)),
            VMEM,
        ],
        out_specs=pl.BlockSpec((K, CZ, CZ), lambda i: (0, i, 0)),
        compiler_params=params(),
        cost_estimate=cost(4),
        name="change",
    )(si, se, spread)
    coupling = pl.pallas_call(
        finish_kernel,
        out_shape=shape(NB, K, K),
        in_specs=[SMEM] + [VMEM] * 3,
        out_specs=VMEM,
        compiler_params=params(),
        cost_estimate=cost(1),
        name="finish",
    )(scal, total, lnear, lfar)
    return basis.reshape(start_vectors.shape), galerkin[None], coupling[None]


def solution(mesh):
    return jax.shard_map(
        body,
        mesh=mesh,
        in_specs=(
            P(None, ("subdomai", "inner"), None, None),
            P(("subdomai", "inner"), None, None),
            P(("subdomai", "inner"), None, None),
            P("subdomai", None),
            P("subdomai", None),
            P("subdomai", None),
        ),
        out_specs=(
            P(None, ("subdomai", "inner"), None, None),
            P("subdomai", None, None),
            P("subdomai", None, None, None),
        ),
        check_vma=False,
    )
```

time: 509 us -> 100 us (0.20)
  the two profiles are of different devices: /device:TPU:2 before, /device:TPU:1 now
where the time goes in v1:
time: 100 us
  Pallas kernels  51.4 us (51%)
  starting transfers between devices  22.4 us (22%)
  blocking collectives  14.4 us (14%)
  waiting for transfers between devices  8.83 us (9%)
  local copies, waits for them, and re-layouts  2.29 us (2%)
    pallas_call x1, Pallas kernels, body(): pl.pallas_call(interior_kernel, out_shape=(shape(K, INSIDE, CZ), shape(2,...  24 us
    pallas_call x1, Pallas kernels, body(): pl.pallas_call(edge_kernel, out_shape=(shape(2, K, CZ, CZ),) + (shape(WMA...  15.5 us
    all_to_all x1, blocking collectives, body(): got = lax.all_to_all(msg, 'inner', 0, 0)  14.4 us
    ppermute x8, starting transfers between devices, swap(): lax.ppermute(x, 'subdomai', [(i, i ^ bits) for i in range(lax.axis_size('...  13.4 us
    ppermute x8, waiting for transfers between devices, swap(): lax.ppermute(x, 'subdomai', [(i, i ^ bits) for i in range(lax.axis_size('...  8.83 us
    ppermute x1, starting transfers between devices, body(): lax.ppermute(down, 'inner', [(i, (i - 1) % groups) for i in range(groups)])  6.82 us
    pallas_call x1, Pallas kernels, body(): pl.pallas_call(change_kernel, out_shape=shape(K, SLAB, CZ), grid=(SLAB //...  4.33 us
    pallas_call x1, Pallas kernels, body(): pl.pallas_call(pack_kernel, out_shape=(shape(PACK, CZ),) * 2, in_specs=[A...  2.82 us
  transfers between devices with their start and end apart: 10, of which 6 were waited for; matrix products, arithmetic and copies ran while one was open for 0% of the time, Pallas kernels for 28%

profile of v1, /device:TPU:1, one launch (start us, length us, event | category | flops | bytes accessed | tf_op | source)
XLA Modules:
  0.0 100.2 jit_solution(5344070371190390998)
XLA Ops:
  0.6 0.0 copy-start.2
  0.6 0.0 copy-start.1
  0.7 0.0 copy-start.5
  0.7 0.0 copy-start.4
  0.7 0.0 copy-start.3
  0.7 2.8 %pack.1 = (f32[1536,128]{1,0:T(8,128)}, f32[1536,128]{1,0:T(8,128)}) custom-call(f32[8,1024,128]{2,1,0:T(8,128)} %bitcast.19, f32[1024,128]{1,0:T(8,128)} %bitcast.22, f32[1024,128]{1,0:T(8,128)} %bitcast.25), custom_call_target="tpu_custom_call" | custom-call | tf_op jit(solution)/shard_map/pack/pallas_call | solution.py:468
  3.5 2.2 %collective-permute-start = (f32[1536,128]{1,0:T(8,128)}, f32[1536,128]{1,0:T(8,128)S(1)}, u32[]{:S(2)}, u32[]{:S(2)}) collective-permute-start(f32[1536,128]{1,0:T(8,128)} %get-tuple-element.20), channel_id=1, source_target_pairs={{0,1},{1,2},{2,3},{3,4},{4,5},{5,6},{6,7},{7,8},{8,9},{9,10},{10,1... | collective-permute-start | bytes 2359304 | tf_op jit(solution)/shard_map/ppermute | solution.py:477
  5.7 6.8 %collective-permute-start.1 = (f32[1536,128]{1,0:T(8,128)}, f32[1536,128]{1,0:T(8,128)S(1)}, u32[]{:S(2)}, u32[]{:S(2)}) collective-permute-start(f32[1536,128]{1,0:T(8,128)} %get-tuple-element.21), channel_id=1, source_target_pairs={{0,31},{1,0},{2,1},{3,2},{4,3},{5,4},{6,5},{7,6},{8,7},{9,8},{10,9... | collective-permute-start | bytes 2359304 | tf_op jit(solution)/shard_map/ppermute | solution.py:476
  12.5 0.0 copy-done.5
  12.5 0.0 copy-done.4
  12.6 0.0 copy-done.3
  12.6 0.1 concatenate.3.scal
  12.6 0.0 copy-done.2
  12.7 0.0 copy-done.1
  12.7 0.0 copy-start
  12.7 2.2 %copy-done = f32[8,16,64,128]{3,2,1,0:T(8,128)S(1)} copy-done((f32[8,16,64,128]{3,2,1,0:T(8,128)S(1)}, f32[8,16,64,128]{3,2,1,0:T(8,128)}, u32[]{:S(2)}) %copy-start) | copy-done | bytes 4194328
  14.9 24.0 %interior.1 = (f32[8,768,128]{2,1,0:T(8,128)S(1)}, f32[2,8,128,128]{3,2,1,0:T(8,128)S(1)}, f32[36,8,128]{2,1,0:T(8,128)S(1)}, f32[36,8,128]{2,1,0:T(8,128)S(1)},...) custom-call(s32[32]{0:T(128)S(1)} %concatenate.3.scal, f32[8,1024,128]{2,1,0:T(8,128)S(1)} %bitcast.20, ...), custom_call_target="tpu_custom_call" | custom-call | bytes 30000000 | tf_op jit(solution)/shard_map/interior/pallas_call | solution.py:481
  38.9 0.0 collective-permute-done.left
  38.9 0.0 collective-permute-done.1.right
  38.9 15.5 %edge.1 = (f32[2,8,128,128]{3,2,1,0:T(8,128)S(1)}, f32[32,1024]{1,0:T(8,128)S(1)}, f32[32,1024]{1,0:T(8,128)S(1)}, f32[8,128]{1,0:T(8,128)S(1)}) custom-call(s32[32]{0:T(128)S(1)} %concatenate.3.scal, f32[1536,128]{1,0:T(8,128)S(1)} %collective-permute-done.left, f32[1536,128]{1,0:T(8,128)S(1)} %collective-permute-done.1.right, ...), custom_call_target="tpu_custom_call" | custom-call | bytes 9000000 | tf_op jit(solution)/shard_map/edge/pallas_call | solution.py:493
  54.5 2.6 %collective-permute-start.4 = (f32[32,1024]{1,0:T(8,128)S(1)}, f32[32,1024]{1,0:T(8,128)S(1)}, u32[]{:S(2)}, u32[]{:S(2)}) collective-permute-start(f32[32,1024]{1,0:T(8,128)S(1)} %get-tuple-element.29), channel_id=1, source_target_pairs={{0,192},{32,224},{64,128},{96,160},{128,64},{160,96},{192,0},{224,... | collective-permute-start | bytes 393224 | tf_op jit(solution)/shard_map/ppermute | solution.py:441
  57.0 0.5 collective-permute-start.3
  57.6 0.3 collective-permute-start.2
  57.8 4.1 %collective-permute-done.4 = f32[32,1024]{1,0:T(8,128)S(1)} collective-permute-done((f32[32,1024]{1,0:T(8,128)S(1)}, f32[32,1024]{1,0:T(8,128)S(1)}, u32[]{:S(2)}, u32[]{:S(2)}) %collective-permute-start.4) | collective-permute-done | bytes 131104 | tf_op jit(solution)/shard_map/ppermute | solution.py:441
  61.9 0.5 collective-permute-done.3
  62.4 0.3 collective-permute-done.2
  62.8 3.2 %collective-permute-start.5 = (f32[4,32,1024]{2,1,0:T(8,128)S(1)}, f32[4,32,1024]{2,1,0:T(8,128)S(1)}, u32[]{:S(2)}, u32[]{:S(2)}) collective-permute-start(f32[4,32,1024]{2,1,0:T(8,128)S(1)} %pad_maximum_fusion.near), channel_id=1, source_target_pairs={{0,32},{32,0},{64,96},{96,64},{128,160},{160,128},{192,224},{224,1... | collective-permute-start | bytes 1572872 | tf_op jit(solution)/shard_map/ppermute | solution.py:441
  66.0 1.5 %collective-permute-done.5.far = f32[4,32,1024]{2,1,0:T(8,128)S(1)} collective-permute-done((f32[4,32,1024]{2,1,0:T(8,128)S(1)}, f32[4,32,1024]{2,1,0:T(8,128)S(1)}, u32[]{:S(2)}, u32[]{:S(2)}) %collective-permute-start.5) | collective-permute-done | bytes 524320 | tf_op jit(solution)/shard_map/ppermute | solution.py:441
  67.5 1.5 %couple.1 = f32[32,8,128]{2,1,0:T(8,128)S(1)} custom-call(s32[32]{0:T(128)S(1)} %concatenate.3.scal, f32[32,1024]{1,0:T(8,128)S(1)} %get-tuple-element.28.window, f32[4,32,1024]{2,1,0:T(8,128)S(1)} %pad_maximum_fusion.near, f32[4,32,1024]{2,1,0:T(8,128)S(1)} %collective-permute-done.5.far, f32[8,128]{1,0:T(8,128)S(1)} %get-tuple-element.30.part), custom_call_target="tpu_custom_call" | custom-call | bytes 3000000 | tf_op jit(solution)/shard_map/couple/pallas_call | solution.py:507
  69.0 14.4 %all_to_all.5.got = f32[32,8,128]{2,1,0:T(8,128)S(1)} all-to-all(f32[32,8,128]{2,1,0:T(8,128)S(1)} %couple.1), channel_id=1, replica_groups=mesh['subdomai'=8,'inner'=32] {'inner'}, dimensions={0} | all-to-all | bytes 262144 | tf_op jit(solution)/shard_map/all_to_all | solution.py:517
  83.5 1.7 %factor.1 = (f32[8,128]{1,0:T(8,128)S(1)}, f32[8,128]{1,0:T(8,128)S(1)}, f32[36,8,128]{2,1,0:T(8,128)S(1)}, f32[8,8]{1,0:T(8,128)}) custom-call(f32[32,8,128]{2,1,0:T(8,128)S(1)} %all_to_all.5.got), custom_call_target="tpu_custom_call" | custom-call | bytes 3000000 | tf_op jit(solution)/shard_map/factor/pallas_call | solution.py:518
  85.1 1.7 %collective-permute-start.8 = (f32[8,128]{1,0:T(8,128)S(1)}, f32[8,128]{1,0:T(8,128)S(1)}, u32[]{:S(2)}, u32[]{:S(2)}) collective-permute-start(f32[8,128]{1,0:T(8,128)S(1)} %get-tuple-element.34), channel_id=1, source_target_pairs={{0,192},{32,224},{64,128},{96,160},{128,64},{160,96},{192,0},{224,... | collective-permute-start | bytes 12296 | tf_op jit(solution)/shard_map/ppermute | solution.py:441
  86.8 0.5 collective-permute-start.7
  87.4 1.0 %collective-permute-start.6 = (f32[8,128]{1,0:T(8,128)S(1)}, f32[8,128]{1,0:T(8,128)S(1)}, u32[]{:S(2)}, u32[]{:S(2)}) collective-permute-start(f32[8,128]{1,0:T(8,128)S(1)} %get-tuple-element.34), channel_id=1, source_target_pairs={{0,64},{32,96},{64,0},{96,32},{128,192},{160,224},{192,128},{224,1... | collective-permute-start | bytes 12296 | tf_op jit(solution)/shard_map/ppermute | solution.py:441
  88.4 0.4 collective-permute-done.8
  88.8 2.0 %collective-permute-done.7 = f32[8,128]{1,0:T(8,128)S(1)} collective-permute-done((f32[8,128]{1,0:T(8,128)S(1)}, f32[8,128]{1,0:T(8,128)S(1)}, u32[]{:S(2)}, u32[]{:S(2)}) %collective-permute-start.7) | collective-permute-done | bytes 4128 | tf_op jit(solution)/shard_map/ppermute | solution.py:441
  90.8 0.0 collective-permute-done.6
  90.8 3.5 %collective-permute-start.9 = (f32[4,8,128]{2,1,0:T(8,128)S(1)}, f32[4,8,128]{2,1,0:T(8,128)S(1)}, u32[]{:S(2)}, u32[]{:S(2)}) collective-permute-start(f32[4,8,128]{2,1,0:T(8,128)S(1)} %pad_maximum_fusion.1.near), channel_id=1, source_target_pairs={{0,32},{32,0},{64,96},{96,64},{128,160},{160,128},{192,224},{224,1... | collective-permute-start | bytes 49160 | tf_op jit(solution)/shard_map/ppermute | solution.py:441
  94.3 4.3 %change.1 = f32[8,1024,128]{2,1,0:T(8,128)} custom-call(f32[8,768,128]{2,1,0:T(8,128)S(1)} %get-tuple-element.19.si, f32[2,8,128,128]{3,2,1,0:T(8,128)S(1)} %get-tuple-element.27.se, f32[36,8,128]{2,1,0:T(8,128)S(1)} %get-tuple-element.31.spread), custom_call_target="tpu_custom_call" | custom-call | bytes 12000000 | tf_op jit(solution)/shard_map/change/pallas_call | solution.py:528
  98.7 0.0 collective-permute-done.9.far
  98.7 1.6 %finish.1 = f32[6,8,8]{2,1,0:T(8,128)} custom-call(s32[32]{0:T(128)S(1)} %concatenate.3.scal, f32[8,128]{1,0:T(8,128)S(1)} %get-tuple-element.33.total, f32[4,8,128]{2,1,0:T(8,128)S(1)} %pad_maximum_fusion.1.near, f32[4,8,128]{2,1,0:T(8,128)S(1)} %collective-permute-done.9.far), custom_call_target="tpu_custom_call" | custom-call | bytes 3000000 | tf_op jit(solution)/shard_map/finish/pallas_call | solution.py:542
  (5 shorter events, 0.0 us)
Async XLA Ops:
  0.6 12.0 %copy-start.2 = (f32[16,64,128]{2,1,0:T(8,128)S(1)}, f32[16,64,128]{2,1,0:T(8,128)}, u32[]{:S(2)}) copy-start(f32[16,64,128]{2,1,0:T(8,128)} %param.8) | copy-start | bytes 1572868
  0.6 12.0 %copy-start.1 = (f32[16,64,128]{2,1,0:T(8,128)S(1)}, f32[16,64,128]{2,1,0:T(8,128)}, u32[]{:S(2)}) copy-start(f32[16,64,128]{2,1,0:T(8,128)} %param.7) | copy-start | bytes 1572868
  0.7 11.9 %copy-start.5 = (s32[1,6]{1,0:T(1,128)S(1)}, s32[1,6]{1,0:T(1,128)}, u32[]{:S(2)}) copy-start(s32[1,6]{1,0:T(1,128)} %param.11) | copy-start | bytes 76
  0.7 11.9 %copy-start.4 = (s32[1,6]{1,0:T(1,128)S(1)}, s32[1,6]{1,0:T(1,128)}, u32[]{:S(2)}) copy-start(s32[1,6]{1,0:T(1,128)} %param.10) | copy-start | bytes 76
  0.7 11.9 %copy-start.3 = (s32[1,2]{1,0:T(1,128)S(1)}, s32[1,2]{1,0:T(1,128)}, u32[]{:S(2)}) copy-start(s32[1,2]{1,0:T(1,128)} %param.9) | copy-start | bytes 28
  3.5 35.4 %collective-permute-start = (f32[1536,128]{1,0:T(8,128)}, f32[1536,128]{1,0:T(8,128)S(1)}, u32[]{:S(2)}, u32[]{:S(2)}) collective-permute-start(f32[1536,128]{1,0:T(8,128)} %get-tuple-element.20), channel_id=1, source_target_pairs={{0,1},{1,2},{2,3},{3,4},{4,5},{5,6},{6,7},{7,8},{8,9},{9,10},{10,1... | collective-permute-start | bytes 2359304 | tf_op jit(solution)/shard_map/ppermute | solution.py:477
  5.7 33.2 %collective-permute-start.1 = (f32[1536,128]{1,0:T(8,128)}, f32[1536,128]{1,0:T(8,128)S(1)}, u32[]{:S(2)}, u32[]{:S(2)}) collective-permute-start(f32[1536,128]{1,0:T(8,128)} %get-tuple-element.21), channel_id=1, source_target_pairs={{0,31},{1,0},{2,1},{3,2},{4,3},{5,4},{6,5},{7,6},{8,7},{9,8},{10,9... | collective-permute-start | bytes 2359304 | tf_op jit(solution)/shard_map/ppermute | solution.py:476
  12.7 2.2 %copy-start = (f32[8,16,64,128]{3,2,1,0:T(8,128)S(1)}, f32[8,16,64,128]{3,2,1,0:T(8,128)}, u32[]{:S(2)}) copy-start(f32[8,16,64,128]{3,2,1,0:T(8,128)} %param.6) | copy-start | bytes 12582916
  54.5 7.5 %collective-permute-start.4 = (f32[32,1024]{1,0:T(8,128)S(1)}, f32[32,1024]{1,0:T(8,128)S(1)}, u32[]{:S(2)}, u32[]{:S(2)}) collective-permute-start(f32[32,1024]{1,0:T(8,128)S(1)} %get-tuple-element.29), channel_id=1, source_target_pairs={{0,192},{32,224},{64,128},{96,160},{128,64},{160,96},{192,0},{224,... | collective-permute-start | bytes 393224 | tf_op jit(solution)/shard_map/ppermute | solution.py:441
  57.0 5.4 %collective-permute-start.3 = (f32[32,1024]{1,0:T(8,128)S(1)}, f32[32,1024]{1,0:T(8,128)S(1)}, u32[]{:S(2)}, u32[]{:S(2)}) collective-permute-start(f32[32,1024]{1,0:T(8,128)S(1)} %get-tuple-element.29), channel_id=1, source_target_pairs={{0,128},{32,160},{64,192},{96,224},{128,0},{160,32},{192,64},{224,... | collective-permute-start | bytes 393224 | tf_op jit(solution)/shard_map/ppermute | solution.py:441
  57.6 5.1 %collective-permute-start.2 = (f32[32,1024]{1,0:T(8,128)S(1)}, f32[32,1024]{1,0:T(8,128)S(1)}, u32[]{:S(2)}, u32[]{:S(2)}) collective-permute-start(f32[32,1024]{1,0:T(8,128)S(1)} %get-tuple-element.29), channel_id=1, source_target_pairs={{0,64},{32,96},{64,0},{96,32},{128,192},{160,224},{192,128},{224,1... | collective-permute-start | bytes 393224 | tf_op jit(solution)/shard_map/ppermute | solution.py:441
  62.8 4.8 %collective-permute-start.5 = (f32[4,32,1024]{2,1,0:T(8,128)S(1)}, f32[4,32,1024]{2,1,0:T(8,128)S(1)}, u32[]{:S(2)}, u32[]{:S(2)}) collective-permute-start(f32[4,32,1024]{2,1,0:T(8,128)S(1)} %pad_maximum_fusion.near), channel_id=1, source_target_pairs={{0,32},{32,0},{64,96},{96,64},{128,160},{160,128},{192,224},{224,1... | collective-permute-start | bytes 1572872 | tf_op jit(solution)/shard_map/ppermute | solution.py:441
  85.1 3.7 %collective-permute-start.8 = (f32[8,128]{1,0:T(8,128)S(1)}, f32[8,128]{1,0:T(8,128)S(1)}, u32[]{:S(2)}, u32[]{:S(2)}) collective-permute-start(f32[8,128]{1,0:T(8,128)S(1)} %get-tuple-element.34), channel_id=1, source_target_pairs={{0,192},{32,224},{64,128},{96,160},{128,64},{160,96},{192,0},{224,... | collective-permute-start | bytes 12296 | tf_op jit(solution)/shard_map/ppermute | solution.py:441
  86.8 4.0 %collective-permute-start.7 = (f32[8,128]{1,0:T(8,128)S(1)}, f32[8,128]{1,0:T(8,128)S(1)}, u32[]{:S(2)}, u32[]{:S(2)}) collective-permute-start(f32[8,128]{1,0:T(8,128)S(1)} %get-tuple-element.34), channel_id=1, source_target_pairs={{0,128},{32,160},{64,192},{96,224},{128,0},{160,32},{192,64},{224,... | collective-permute-start | bytes 12296 | tf_op jit(solution)/shard_map/ppermute | solution.py:441
  87.4 3.4 %collective-permute-start.6 = (f32[8,128]{1,0:T(8,128)S(1)}, f32[8,128]{1,0:T(8,128)S(1)}, u32[]{:S(2)}, u32[]{:S(2)}) collective-permute-start(f32[8,128]{1,0:T(8,128)S(1)} %get-tuple-element.34), channel_id=1, source_target_pairs={{0,64},{32,96},{64,0},{96,32},{128,192},{160,224},{192,128},{224,1... | collective-permute-start | bytes 12296 | tf_op jit(solution)/shard_map/ppermute | solution.py:441
  90.8 7.9 %collective-permute-start.9 = (f32[4,8,128]{2,1,0:T(8,128)S(1)}, f32[4,8,128]{2,1,0:T(8,128)S(1)}, u32[]{:S(2)}, u32[]{:S(2)}) collective-permute-start(f32[4,8,128]{2,1,0:T(8,128)S(1)} %pad_maximum_fusion.1.near), channel_id=1, source_target_pairs={{0,32},{32,0},{64,96},{96,64},{128,160},{160,128},{192,224},{224,1... | collective-permute-start | bytes 49160 | tf_op jit(solution)/shard_map/ppermute | solution.py:441

commit v2 on v1

v2 whole, which is shorter than its diff:
```python
import functools
import jax
import jax.numpy as jnp
from jax import lax
from jax.experimental import pallas as pl
from jax.experimental.pallas import tpu as pltpu
from jax.sharding import PartitionSpec as P

F32 = jnp.float32
K = 8
NB = 6
SUBDOMAINS = 8
WMAX = 4
CY = 64
CZ = 128
OMEGA = 0.6
SLAB = 16 * CY
HALO = 160
HALO_ACC = 96
OFF = HALO + 8
RT = SLAB + 2 * OFF
PACK = K * HALO + HALO + HALO_ACC
PAIRS = [(a, b) for b in range(K) for a in range(b + 1)]
NP = len(PAIRS)
HIGHEST = lax.Precision.HIGHEST
VMEM = pl.BlockSpec(memory_space=pltpu.VMEM)
SMEM = pl.BlockSpec(memory_space=pltpu.SMEM)
HBM = pl.BlockSpec(memory_space=pltpu.HBM)
ANY = pl.BlockSpec(memory_space=pl.ANY)


def shape(*dims):
    return jax.ShapeDtypeStruct(dims, F32)


def rows_loop(lo, hi, step, init=(), tiles=4):
    def one(i, carry):
        stores = []
        for j in range(tiles):
            more, carry = step(pl.multiple_of(lo + OFF + (i * tiles + j) * 8, 8), carry)
            stores += more
        for ref, place, value in stores:
            ref[place] = value
        return carry

    assert (hi - lo) % (8 * tiles) == 0
    return lax.fori_loop(0, (hi - lo) // (8 * tiles), one, init)


def tile_at(row):
    return (pl.ds(row, 8), slice(None))


def field_at(a, row):
    return (a, pl.ds(row, 8), slice(None))


def lanes():
    return lax.broadcasted_iota(jnp.int32, (8, CZ), 1)


def sublanes():
    return lax.broadcasted_iota(jnp.int32, (8, CZ), 0)


def at(ref, row):
    return ref[pl.ds(row, 8), :]


def fat(ref, a, row):
    return ref[a, pl.ds(row, 8), :]


def layer_of(row):
    return lax.shift_right_arithmetic(row + (192 - OFF), 6) - 3


def active(scal, row, more=0):
    x = scal[2] + layer_of(row) + more
    return jnp.where((x >= 0) & (x < scal[0]), 1.0, 0.0).astype(F32)


def faces(scal, kp, fx, fy, fz, lo, hi, tiles=8):
    mz = jnp.where(lanes() < scal[1], 2.0, 0.0).astype(F32)
    mzz = jnp.where(lanes() < scal[1] - 1, 2.0, 0.0).astype(F32)
    sub = sublanes()

    def step(r, carry):
        here = active(scal, r)
        there = active(scal, r, 1)
        k = at(kp, r)
        kx = at(kp, r + CY)
        ky = at(kp, r + 1)
        kz = pltpu.roll(k, CZ - 1, 1)
        inside = jnp.where(((r + (192 - OFF)) & (CY - 1)) == CY - 8, 0.0, 1.0).astype(F32)
        my = jnp.where(sub == 7, inside, 1.0)
        stores = [
            (fx, tile_at(r), (mz * (here * there)) * k * kx / (k + kx)),
            (fy, tile_at(r), (mz * here) * my * k * ky / (k + ky)),
            (fz, tile_at(r), (mzz * here) * k * kz / (k + kz)),
        ]
        return stores, carry

    rows_loop(lo, hi, step, tiles=tiles)


def weights(ac, fx, fy, fz, w, lo, hi, tiles=8):
    def step(r, carry):
        z = at(fz, r)
        diagonal = (
            (at(ac, r) + at(fx, r))
            + (at(fx, r - CY) + at(fy, r))
            + (at(fy, r - 1) + z)
            + pltpu.roll(z, 1, 1)
        )
        return [(w, tile_at(r), OMEGA / diagonal)], carry

    rows_loop(lo, hi, step, tiles=tiles)


def smooth(scal, src, dst, fx, fy, fz, w, lo, hi, masked, tiles=16, back=0):
    mz = jnp.where(lanes() < scal[1], 1.0 - OMEGA, 0.0).astype(F32)

    def step(r, carry):
        wt = at(w, r)
        z = at(fz, r)
        xp = wt * at(fx, r)
        xm = wt * at(fx, r - CY)
        yp = wt * at(fy, r)
        ym = wt * at(fy, r - 1)
        zp = wt * z
        zm = wt * pltpu.roll(z, 1, 1)
        centre = mz * active(scal, r) if masked else 1.0 - OMEGA
        stores = []
        for a in range(K):
            v = fat(src, a, r)
            new = (
                (centre * v + xp * fat(src, a, r + CY))
                + (xm * fat(src, a, r - CY) + yp * fat(src, a, r + 1))
                + (ym * fat(src, a, r - 1) + zp * pltpu.roll(v, CZ - 1, 1))
                + zm * pltpu.roll(v, 1, 1)
            )
            stores.append((dst, field_at(a, r - back), new))
        return stores, carry

    rows_loop(lo, hi, step, tiles=tiles)


def gram_sums(s, lo, hi, acc, back=0):
    def step(r, acc):
        v = [fat(s, a, r - back) for a in range(K)]
        return [], tuple(t + v[a] * v[b] for t, (a, b) in zip(acc, PAIRS))

    return rows_loop(lo, hi, step, tuple(acc), tiles=4)


def flux_sums(s, ac, fx, fy, fz, lo, hi, acc, before=True, after=True, back=0):
    def step(r, acc):
        out = list(acc)
        z = at(fz, r)
        xp = at(fx, r)
        xm = at(fx, r - CY)
        yp = at(fy, r)
        ym = at(fy, r - 1)
        d = at(ac, r)
        q = r - back
        v = [fat(s, a, q) for a in range(K)]
        g = [c - pltpu.roll(c, CZ - 1, 1) for c in v]
        for b in range(K):
            c = v[b]
            image = d * c + yp * (c - fat(s, b, q + 1)) + ym * (c - fat(s, b, q - 1))
            if after:
                image = image + xp * (c - fat(s, b, q + CY))
            if before:
                image = image + xm * (c - fat(s, b, q - CY))
            down = z * g[b]
            for a in range(b + 1):
                p = b * (b + 1) // 2 + a
                out[p] = out[p] + (v[a] * image + g[a] * down)
        return [], tuple(out)

    return rows_loop(lo, hi, step, tuple(acc), tiles=4)


def crossing_sums(s, fx, lo, hi, acc):
    def step(r, acc):
        f = at(fx, r)
        d = [fat(s, a, r) - fat(s, a, r + CY) for a in range(K)]
        e = [f * t for t in d]
        return [], tuple(t + d[a] * e[b] for t, (a, b) in zip(acc, PAIRS))

    return rows_loop(lo, hi, step, tuple(acc), tiles=1)


def turned(scal, s, kp, first, window, tile, ptile, blocks, back=0):
    start = scal[1] - WMAX

    def step(block, row, lane):
        ptile[...] = kp[pl.ds(row, CZ), :].T
        kw = ptile[pl.ds(start, WMAX), :]
        for a in range(K):
            tile[a] = s[a, pl.ds(pl.multiple_of(row - back, 8), CZ), :].T
        for a in range(K):
            u = tile[a, pl.ds(start, WMAX), :] * kw
            f = tile[a, pl.ds(0, WMAX), :]
            for t in range(WMAX):
                first[pl.ds(t * K + a, 1), pl.ds(lane, CZ)] = f[t : t + 1]
                window[pl.ds(t * K + a, 1), pl.ds(lane, CZ)] = u[t : t + 1]

    def one(block, carry):
        step(block, pl.multiple_of(OFF + block * CZ, 8), pl.multiple_of((block - blocks[0]) * CZ, CZ))
        return carry

    lax.fori_loop(blocks[0], blocks[1], one, 0)


def copy_all(pairs, sem):
    copies = [pltpu.make_async_copy(src, dst, sem.at[i]) for i, (src, dst) in enumerate(pairs)]
    for c in copies:
        c.start()
    return copies


def wait_all(copies):
    for c in copies:
        c.wait()


def pack_kernel(sv, perm, acc, down, up, sem):
    pairs = []
    for out, lo, acc_lo in ((down, 0, 0), (up, SLAB - HALO, SLAB - HALO_ACC)):
        for a in range(K):
            pairs.append((sv.at[a, pl.ds(lo, HALO)], out.at[pl.ds(a * HALO, HALO)]))
        pairs.append((perm.at[pl.ds(lo, HALO)], out.at[pl.ds(K * HALO, HALO)]))
        pairs.append((acc.at[pl.ds(acc_lo, HALO_ACC)], out.at[pl.ds((K + 1) * HALO, HALO_ACC)]))
    wait_all(copy_all(pairs, sem))


INSIDE = SLAB - 4 * CY
EDGE = 2 * CY + 32
FIRST = WMAX * K
SENT = SLAB // CZ * FIRST + 8


BACK = OFF + 2 * CY


def interior_kernel(
    scal, sv, perm, acc, si, ve, fx, fy, fz, w, gram, first, window, v0, v1, kp, ac, tile, ptile, sem
):
    slab = pl.ds(OFF, SLAB)
    a, b, c = copy_all([(perm, kp.at[slab]), (acc, ac.at[slab]), (sv, v0.at[:, slab])], sem)
    a.wait()
    faces(scal, kp, fx, fy, fz, 0, SLAB - CY)
    b.wait()
    weights(ac, fx, fy, fz, w, CY, SLAB - CY)
    c.wait()
    smooth(scal, v0, v1, fx, fy, fz, w, CY, SLAB - CY, True)
    out = copy_all(
        [
            (v0.at[:, pl.ds(OFF, CZ)], ve.at[0]),
            (v0.at[:, pl.ds(OFF + SLAB - CZ, CZ)], ve.at[1]),
            (v1.at[:, pl.ds(OFF + CY, CZ)], ve.at[2]),
            (v1.at[:, pl.ds(OFF + SLAB - CY - CZ, CZ)], ve.at[3]),
        ],
        sem,
    )
    smooth(scal, v1, si, fx, fy, fz, w, 2 * CY, SLAB - 2 * CY, False, back=BACK)
    zero = [jnp.zeros((8, CZ), F32)] * NP
    for i, t in enumerate(gram_sums(si, 2 * CY, SLAB - 2 * CY, zero, back=BACK)):
        gram[i] = t
    turned(scal, si, kp, first, window, tile, ptile, (1, 7), back=BACK)
    wait_all(out)


def edge_kernel(
    scal, left, right, perm, acc, ve, fxi, fyi, fzi, wi, gram, firsti, windowi,
    se, sent, window, fx, fy, fz, v0, v1, s, kp, ac, w, fe, we, tile, ptile, sem,
):
    pairs = []
    own = SLAB - CZ
    for src, lo, acc_lo, near in ((left, -HALO, -HALO_ACC, 0), (right, SLAB, SLAB, own)):
        pairs.append((src.at[pl.ds(K * HALO, HALO)], kp.at[pl.ds(OFF + lo, HALO)]))
        pairs.append((src.at[pl.ds((K + 1) * HALO, HALO_ACC)], ac.at[pl.ds(OFF + acc_lo, HALO_ACC)]))
        pairs.append((perm.at[pl.ds(near, CZ)], kp.at[pl.ds(OFF + near, CZ)]))
        pairs.append((acc.at[pl.ds(near, CZ)], ac.at[pl.ds(OFF + near, CZ)]))
    early = len(pairs)
    for src, lo in ((left, -HALO), (right, SLAB)):
        for a in range(K):
            pairs.append((src.at[pl.ds(a * HALO, HALO)], v0.at[a, pl.ds(OFF + lo, HALO)]))
    for old, new in ((fxi, fx), (fyi, fy), (fzi, fz)):
        for near, count in ((0, 3 * CY), (SLAB - 4 * CY, 3 * CY)):
            rows = pl.ds(OFF + near, count)
            pairs.append((old.at[rows], new.at[rows]))
    for near in (CY, SLAB - 2 * CY):
        rows = pl.ds(OFF + near, CY)
        pairs.append((wi.at[rows], w.at[rows]))
    pairs.append((ve.at[0], v0.at[:, pl.ds(OFF, CZ)]))
    pairs.append((ve.at[1], v0.at[:, pl.ds(OFF + own, CZ)]))
    pairs.append((ve.at[2], v1.at[:, pl.ds(OFF + CY, CZ)]))
    pairs.append((ve.at[3], v1.at[:, pl.ds(OFF + SLAB - CY - CZ, CZ)]))
    copies = copy_all(pairs, sem)
    wait_all(copies[:early])
    wait_all(copies[early:])
    faces(scal, kp, fx, fy, fz, -HALO, 0, 20)
    faces(scal, kp, fx, fy, fz, SLAB - CY, SLAB + HALO_ACC, 20)
    weights(ac, fx, fy, fz, w, -HALO_ACC, CY, 20)
    weights(ac, fx, fy, fz, w, SLAB - CY, SLAB + HALO_ACC, 20)
    smooth(scal, v0, v1, fx, fy, fz, w, -HALO_ACC, CY, True, 20)
    smooth(scal, v0, v1, fx, fy, fz, w, SLAB - CY, SLAB + HALO_ACC, True, 20)
    smooth(scal, v1, s, fx, fy, fz, w, -32, 2 * CY, False, 20)
    smooth(scal, v1, s, fx, fy, fz, w, SLAB - 2 * CY, SLAB + 32, False, 20)
    out = copy_all(
        [
            (s.at[:, pl.ds(OFF - 32, EDGE)], se.at[0]),
            (s.at[:, pl.ds(OFF + own, EDGE)], se.at[1]),
        ],
        sem,
    )
    window[:, pl.ds(CZ, INSIDE)] = windowi[...]
    for i in range(INSIDE // CZ):
        sent[pl.ds((i + 1) * FIRST, FIRST), :] = firsti[:, i * CZ : (i + 1) * CZ]
    for i, lane in ((0, 0), (7, own)):
        turned(scal, s, kp, fe, we, tile, ptile, (i, i + 1))
        sent[pl.ds(i * FIRST, FIRST), :] = fe[...]
        window[:, pl.ds(lane, CZ)] = we[...]
    acc = [gram[i] for i in range(NP)]
    acc = gram_sums(s, 0, 2 * CY, acc)
    acc = gram_sums(s, SLAB - 2 * CY, SLAB, acc)
    lane = lanes()
    res = jnp.zeros((8, CZ), F32)
    for b, col in enumerate(lane_sums(acc)):
        res = jnp.where(lane == b, col, res)
    sent[pl.ds(SENT - 8, 8), :] = res
    wait_all(out)


def flux_kernel(se, si, acc, fxi, fyi, fzi, fx, fy, fz, part, s, ac, sem):
    own = SLAB - CZ
    wait_all(
        copy_all(
            [
                (se.at[0], s.at[:, pl.ds(OFF - 32, EDGE)]),
                (se.at[1], s.at[:, pl.ds(OFF + own, EDGE)]),
                (si.at[:, pl.ds(0, CZ)], s.at[:, pl.ds(OFF + CZ, CZ)]),
                (si.at[:, pl.ds(INSIDE - CZ, CZ)], s.at[:, pl.ds(OFF + own - CZ, CZ)]),
                (acc, ac.at[pl.ds(OFF, SLAB)]),
            ],
            sem,
        )
    )
    acc = [jnp.zeros((8, CZ), F32)] * NP
    acc = flux_sums(si, ac, fxi, fyi, fzi, 3 * CY, SLAB - 3 * CY, acc, back=BACK)
    acc = flux_sums(s, ac, fx, fy, fz, 0, CY, acc, before=False)
    acc = flux_sums(s, ac, fx, fy, fz, CY, 3 * CY, acc)
    acc = flux_sums(s, ac, fx, fy, fz, SLAB - 3 * CY, SLAB - CY, acc)
    acc = flux_sums(s, ac, fx, fy, fz, SLAB - CY, SLAB, acc, after=False)
    acc = crossing_sums(s, fx, -32, 0, acc)
    acc = crossing_sums(s, fx, SLAB - CY, SLAB - 32, acc)
    lane = lanes()
    res = jnp.zeros((8, CZ), F32)
    for b, col in enumerate(lane_sums(acc)):
        res = jnp.where(lane == b, col, res)
    part[...] = res


def lane_sums(acc):
    row = sublanes()
    cols = []
    for b in range(K):
        x = jnp.zeros((8, CZ), F32)
        for a in range(K):
            p = PAIRS.index((min(a, b), max(a, b)))
            x = jnp.where(row == a, jnp.sum(acc[p], axis=0, keepdims=True), x)
        cols.append(jnp.sum(x, axis=1, keepdims=True))
    return cols


GRAM = NB * K
FLUX = GRAM + K
OTHERS = FLUX + K


def couple_kernel(scal, window, near, far, part, msg, chosen, prod):
    for n in range(NB):
        m = scal[8 + n] ^ scal[3]
        place = lax.shift_right_logical(m, 1)
        odd = (m & 1) == 1
        for i in range(SLAB // CZ):
            for t in range(WMAX):
                rows = pl.ds(i * FIRST + t * K, K)
                value = jnp.where(odd, far[place, rows, :], near[place, rows, :])
                chosen[pl.ds((t * NB + n) * K, K), i * CZ : (i + 1) * CZ] = value
    prod[:, : WMAX * NB * K] = lax.dot_general(
        window[...], chosen[...], (((1,), (1,)), ((), ())), precision=HIGHEST, preferred_element_type=F32
    )
    lane = lax.broadcasted_iota(jnp.int32, (8, 2 * CZ), 1)
    total = jnp.zeros((8, 2 * CZ), F32)
    for t in range(WMAX):
        x = jnp.zeros((8, 2 * CZ), F32)
        for n in range(NB):
            width = scal[16 + n]
            d = jnp.where(t < width, WMAX - width + t, 0)
            v = prod[pl.ds(pl.multiple_of(d * K, K), K), :]
            lo = (t * NB + n) * K
            keep = (lane >= lo) & (lane < lo + K) & (t < width)
            x = jnp.where(keep, v, x)
        total = total + (pltpu.roll(x, 2 * CZ - t * NB * K, 1) if t else x)
    lane = lanes()
    res = jnp.where(lane < GRAM, total[:, :CZ], 0.0)
    res = res + pltpu.roll(part[...], FLUX, 1)
    for m in range(SUBDOMAINS):
        g = (far if m & 1 else near)[m // 2, pl.ds(SENT - 8, 8), :]
        res = res + pltpu.roll(g, OTHERS + (m - 1) * K if m else GRAM, 1)
    for i in range(msg.shape[0]):
        msg[i] = res


def eliminate(grams):
    row, lane = sublanes(), lanes()
    column = row[:, :1]
    es = []
    for g in grams:
        e = jnp.where(lane < K, g, jnp.where(lane == row + K, 1.0, 0.0))
        es.append(jnp.where(lane < 2 * K, e, 0.0))
    roots = [jnp.ones((8, 1), F32)] * len(es)
    for k in range(K):
        for m, e in enumerate(es):
            pivot = e[k : k + 1, k : k + 1]
            factor = jnp.where(column > k, e[:, k : k + 1] / pivot, 0.0)
            roots[m] = jnp.where(column == k, 1.0 / jnp.sqrt(pivot), roots[m])
            es[m] = e - factor * e[k : k + 1, :]
    return [jnp.where(lane < K, pltpu.roll(e * root, CZ - K, 1), 0.0) for e, root in zip(es, roots)]


def finish_kernel(scale, scal, got, si, se, basis, galerkin, coupling, inverse, out, sem):
    total = jnp.sum(got[...], axis=0) * scale
    (li,) = eliminate([pltpu.roll(total, CZ - GRAM, 1)])
    inverse[0] = li
    c = {(b, a): jnp.broadcast_to(li[a : a + 1, b : b + 1], (8, CZ)) for b, a in PAIRS}
    copies = []
    for i in range(SLAB // CZ):
        if i == 0:
            src = se.at[0, :, pl.ds(32, CZ)]
        elif i == SLAB // CZ - 1:
            src = se.at[1, :, pl.ds(0, CZ)]
        else:
            src = si.at[:, pl.ds((i - 1) * CZ, CZ)]

        def step(j, carry, src=src, i=i):
            stores = []
            for t in range(4):
                r = pl.multiple_of(j * 32 + t * 8, 8)
                v = [src[a, pl.ds(r, 8), :] for a in range(K)]
                for a in range(K):
                    x = c[0, a] * v[0]
                    for b in range(1, a + 1):
                        x = x + c[b, a] * v[b]
                    stores.append((a, r, x))
            for a, r, x in stores:
                out[i, a, pl.ds(r, 8), :] = x
            return carry

        lax.fori_loop(0, CZ // 32, step, 0)
        copies.append(pltpu.make_async_copy(out.at[i], basis.at[:, pl.ds(i * CZ, CZ)], sem.at[i]))
        copies[-1].start()
    others = eliminate([pltpu.roll(total, CZ - OTHERS - m * K, 1) for m in range(SUBDOMAINS - 1)])
    for m, other in enumerate(others):
        inverse[m + 1] = other
    y = jnp.dot(li[:, :K], total[:, :OTHERS], precision=HIGHEST, preferred_element_type=F32)
    transposed = (((1,), (1,)), ((), ()))
    galerkin[...] = lax.dot_general(
        y[:, FLUX:OTHERS], li[:, :K], transposed, precision=HIGHEST, preferred_element_type=F32
    )
    for n in range(NB):
        other = inverse[scal[8 + n] ^ scal[3]]
        coupling[n] = lax.dot_general(
            y[:, n * K : n * K + K], other[:, :K], transposed, precision=HIGHEST, preferred_element_type=F32
        )
    wait_all(copies)


def params(mib=40):
    return pltpu.CompilerParams(vmem_limit_bytes=mib * 1024 * 1024)


def cost(us):
    return pl.CostEstimate(flops=0, bytes_accessed=int(us * 3.0e6), transcendentals=0)


def swap(x, bits):
    return lax.ppermute(x, "subdomai", [(i, i ^ bits) for i in range(lax.axis_size("subdomai"))])


def body(start_vectors, permeability, accumulation, extents, neighbour_ids, intersection_widths):
    groups = lax.axis_size("inner")
    cells = groups * SLAB * CZ
    inner = lax.axis_index("inner")
    own = lax.axis_index("subdomai")
    sv = start_vectors.reshape(K, SLAB, CZ)
    perm = permeability.reshape(SLAB, CZ)
    acc = accumulation.reshape(SLAB, CZ)
    scal = jnp.concatenate(
        [
            extents[0],
            jnp.stack([inner * 16, own]).astype(jnp.int32),
            jnp.zeros(4, jnp.int32),
            neighbour_ids[0],
            jnp.zeros(2, jnp.int32),
            intersection_widths[0],
            jnp.zeros(10, jnp.int32),
        ]
    )
    down, up = pl.pallas_call(
        pack_kernel,
        out_shape=(shape(PACK, CZ),) * 2,
        in_specs=[HBM] * 3,
        out_specs=(VMEM,) * 2,
        scratch_shapes=[pltpu.SemaphoreType.DMA((20,))],
        compiler_params=params(60),
        name="pack",
    )(sv, perm, acc)
    right = lax.ppermute(down, "inner", [(i, (i - 1) % groups) for i in range(groups)])
    left = lax.ppermute(up, "inner", [(i, (i + 1) % groups) for i in range(groups)])
    field, plain = pltpu.VMEM((K, RT, CZ), F32), pltpu.VMEM((RT, CZ), F32)
    turning = [pltpu.VMEM((K, CZ, CZ), F32), pltpu.VMEM((CZ, CZ), F32)]
    turn = shape(FIRST, INSIDE)
    si, ve, fx, fy, fz, w, gram, first, window = pl.pallas_call(
        interior_kernel,
        out_shape=(shape(K, INSIDE, CZ), shape(4, K, CZ, CZ))
        + (shape(RT, CZ),) * 4
        + (shape(NP, 8, CZ),)
        + (turn,) * 2,
        in_specs=[SMEM, HBM, HBM, HBM],
        out_specs=(VMEM,) * 9,
        scratch_shapes=[field] * 2 + [plain] * 2 + turning + [pltpu.SemaphoreType.DMA((4,))],
        compiler_params=params(40),
        cost_estimate=cost(13),
        name="interior",
    )(scal, sv, perm, acc)
    se, sent, window, fxe, fye, fze = pl.pallas_call(
        edge_kernel,
        out_shape=(shape(2, K, EDGE, CZ), shape(SENT, CZ), shape(FIRST, SLAB)) + (shape(RT, CZ),) * 3,
        in_specs=[SMEM] + [VMEM] * 2 + [HBM] * 2 + [VMEM] * 8,
        out_specs=(VMEM,) * 6,
        scratch_shapes=[field] * 3
        + [plain] * 3
        + [pltpu.VMEM((FIRST, CZ), F32)] * 2
        + turning
        + [pltpu.SemaphoreType.DMA((48,))],
        compiler_params=params(24),
        cost_estimate=cost(6),
        name="edge",
    )(scal, left, right, perm, acc, ve, fx, fy, fz, w, gram, first, window)
    moved = [swap(sent, bits) for bits in (2, 4, 6)]
    part = pl.pallas_call(
        flux_kernel,
        out_shape=shape(8, CZ),
        in_specs=[VMEM] * 2 + [HBM] + [VMEM] * 6,
        out_specs=VMEM,
        scratch_shapes=[field, plain, pltpu.SemaphoreType.DMA((5,))],
        compiler_params=params(10),
        cost_estimate=cost(6),
        name="flux",
    )(se, si, acc, fx, fy, fz, fxe, fye, fze)
    moved, part = lax.optimization_barrier((moved, part))
    near = jnp.stack([sent] + moved)
    far = swap(near, 1)
    msg = pl.pallas_call(
        couple_kernel,
        out_shape=shape(groups, 8, CZ),
        in_specs=[SMEM] + [VMEM] * 4,
        out_specs=VMEM,
        scratch_shapes=[pltpu.VMEM((WMAX * NB * K, SLAB), F32), pltpu.VMEM((FIRST, 2 * CZ), F32)],
        compiler_params=params(8),
        cost_estimate=cost(1),
        name="couple",
    )(scal, window, near, far, part)
    got = lax.all_to_all(msg, "inner", 0, 0)
    basis, galerkin, coupling = pl.pallas_call(
        functools.partial(finish_kernel, 1.0 / cells),
        out_shape=(shape(K, SLAB, CZ), shape(K, K), shape(NB, K, K)),
        in_specs=[SMEM] + [VMEM] * 3,
        out_specs=(HBM, VMEM, VMEM),
        scratch_shapes=[
            pltpu.VMEM((SUBDOMAINS, 8, CZ), F32),
            pltpu.VMEM((SLAB // CZ, K, CZ, CZ), F32),
            pltpu.SemaphoreType.DMA((SLAB // CZ,)),
        ],
        compiler_params=params(8),
        cost_estimate=cost(5),
        name="finish",
    )(scal, got, si, se)
    return basis.reshape(start_vectors.shape), galerkin[None], coupling[None]


def solution(mesh):
    return jax.shard_map(
        body,
        mesh=mesh,
        in_specs=(
            P(None, ("subdomai", "inner"), None, None),
            P(("subdomai", "inner"), None, None),
            P(("subdomai", "inner"), None, None),
            P("subdomai", None),
            P("subdomai", None),
            P("subdomai", None),
        ),
        out_specs=(
            P(None, ("subdomai", "inner"), None, None),
            P("subdomai", None, None),
            P("subdomai", None, None, None),
        ),
        check_vma=False,
    )
```

time: 100 us -> 75.3 us (0.75)
  Pallas kernels: 51.4 us -> 34.5 us
  starting transfers between devices: 22.4 us -> 14.5 us
  waiting for transfers between devices: 8.83 us -> 5.54 us
  blocking collectives: 14.4 us -> 16.9 us
    pallas_call x6 -> x5, Pallas kernels: 50 us -> 32.9 us  [the longest x1 11.1 us: body(): pl.pallas_call(interior_kernel, out_shape=(shape(K, INSIDE, CZ), shape(4,...]
    ppermute x8 -> x4, starting transfers between devices: 13.4 us -> 5.5 us  [swap(): lax.ppermute(x, 'subdomai', [(i, i ^ bits) for i in range(lax.axis_size('...]
    ppermute x8 -> x4, waiting for transfers between devices: 8.83 us -> 1.57 us  [swap(): lax.ppermute(x, 'subdomai', [(i, i ^ bits) for i in range(lax.axis_size('...]
    ppermute x1, waiting for transfers between devices: 0.01 us -> 3.97 us  [body(): lax.ppermute(up, 'inner', [(i, (i + 1) % groups) for i in range(groups)])]
    all_to_all x1, blocking collectives: 14.4 us -> 16.9 us  [body(): got = lax.all_to_all(msg, 'inner', 0, 0)]
  transfers between devices with their start and end apart: 10 -> 6, of which waited for: 6 -> 2; matrix products, arithmetic and copies ran while one was open for 0% -> 0% of each run, Pallas kernels for 28% -> 24%
where the time goes in v2:
time: 75.3 us; the launch traced here: 74.5 us
  Pallas kernels  34.5 us (46%)
  blocking collectives  16.9 us (22%)
  starting transfers between devices  14.5 us (19%)
  waiting for transfers between devices  5.54 us (7%)
  local copies, waits for them, and re-layouts  2.29 us (3%)
  between operations  0.79 us (1%)
    all_to_all x1, blocking collectives, body(): got = lax.all_to_all(msg, 'inner', 0, 0)  16.9 us
    pallas_call x1, Pallas kernels, body(): pl.pallas_call(interior_kernel, out_shape=(shape(K, INSIDE, CZ), shape(4,...  11.1 us
    pallas_call x1, Pallas kernels, body(): pl.pallas_call(edge_kernel, out_shape=(shape(2, K, EDGE, CZ), shape(SENT,...  7.5 us
    ppermute x1, starting transfers between devices, body(): lax.ppermute(down, 'inner', [(i, (i - 1) % groups) for i in range(groups)])  6.82 us
    pallas_call x1, Pallas kernels, body(): pl.pallas_call(flux_kernel, out_shape=shape(8, CZ), in_specs=[VMEM] * 2 +...  6.5 us
    ppermute x4, starting transfers between devices, swap(): lax.ppermute(x, 'subdomai', [(i, i ^ bits) for i in range(lax.axis_size('...  5.5 us
    pallas_call x1, Pallas kernels, body(): pl.pallas_call(functools.partial(finish_kernel, 1.0 / cells), out_shape=(...  5.01 us
    ppermute x1, waiting for transfers between devices, body(): lax.ppermute(up, 'inner', [(i, (i + 1) % groups) for i in range(groups)])  3.97 us
  transfers between devices with their start and end apart: 6, of which 2 were waited for; matrix products, arithmetic and copies ran while one was open for 0% of the time, Pallas kernels for 24%

profile of v2, /device:TPU:1, one launch (start us, length us, event | category | flops | bytes accessed | tf_op | source)
XLA Modules:
  0.0 74.5 jit_solution(12051841408640092234)
XLA Ops:
  0.6 0.0 copy-start.1
  0.6 0.0 copy-start.2
  0.7 0.0 copy-start.5
  0.7 0.0 copy-start.4
  0.7 0.0 copy-start.3
  0.7 2.8 %pack.1 = (f32[1536,128]{1,0:T(8,128)}, f32[1536,128]{1,0:T(8,128)}) custom-call(f32[8,1024,128]{2,1,0:T(8,128)} %bitcast.15, f32[1024,128]{1,0:T(8,128)} %bitcast.21, f32[1024,128]{1,0:T(8,128)} %bitcast.17), custom_call_target="tpu_custom_call" | custom-call | tf_op jit(solution)/shard_map/pack/pallas_call | solution.py:514
  3.5 2.2 %collective-permute-start = (f32[1536,128]{1,0:T(8,128)}, f32[1536,128]{1,0:T(8,128)S(1)}, u32[]{:S(2)}, u32[]{:S(2)}) collective-permute-start(f32[1536,128]{1,0:T(8,128)} %get-tuple-element.27), channel_id=1, source_target_pairs={{0,1},{1,2},{2,3},{3,4},{4,5},{5,6},{6,7},{7,8},{8,9},{9,10},{10,1... | collective-permute-start | bytes 2359304 | tf_op jit(solution)/shard_map/ppermute | solution.py:524
  5.7 6.8 %collective-permute-start.1 = (f32[1536,128]{1,0:T(8,128)}, f32[1536,128]{1,0:T(8,128)S(1)}, u32[]{:S(2)}, u32[]{:S(2)}) collective-permute-start(f32[1536,128]{1,0:T(8,128)} %get-tuple-element.28), channel_id=1, source_target_pairs={{0,31},{1,0},{2,1},{3,2},{4,3},{5,4},{6,5},{7,6},{8,7},{9,8},{10,9... | collective-permute-start | bytes 2359304 | tf_op jit(solution)/shard_map/ppermute | solution.py:523
  12.6 0.0 copy-done.5
  12.6 0.0 copy-done.4
  12.6 0.0 copy-done.3
  12.6 0.1 concatenate.3.scal
  12.7 0.0 copy-done.1
  12.7 0.0 copy-done.2
  12.7 0.0 copy-start
  12.7 2.2 %copy-done = f32[8,16,64,128]{3,2,1,0:T(8,128)S(1)} copy-done((f32[8,16,64,128]{3,2,1,0:T(8,128)S(1)}, f32[8,16,64,128]{3,2,1,0:T(8,128)}, u32[]{:S(2)}) %copy-start) | copy-done | bytes 4194328
  14.9 11.1 %interior.1 = (f32[8,768,128]{2,1,0:T(8,128)S(1)}, f32[4,8,128,128]{3,2,1,0:T(8,128)S(1)}, f32[1360,128]{1,0:T(8,128)S(1)}, f32[1360,128]{1,0:T(8,128)S(1)}, f32...) custom-call(s32[32]{0:T(128)S(1)} %concatenate.3.scal, ...), custom_call_target="tpu_custom_call" | custom-call | bytes 39000000 | tf_op jit(solution)/shard_map/interior/pallas_call | solution.py:528
  26.0 4.0 %collective-permute-done.left = f32[1536,128]{1,0:T(8,128)S(1)} collective-permute-done((f32[1536,128]{1,0:T(8,128)}, f32[1536,128]{1,0:T(8,128)S(1)}, u32[]{:S(2)}, u32[]{:S(2)}) %collective-permute-start) | collective-permute-done | bytes 786464 | tf_op jit(solution)/shard_map/ppermute | solution.py:524
  29.9 0.0 collective-permute-done.1.right
  29.9 7.5 %edge.1 = (f32[2,8,160,128]{3,2,1,0:T(8,128)S(1)}, f32[264,128]{1,0:T(8,128)S(1)}, f32[32,1024]{1,0:T(8,128)S(1)}, f32[1360,128]{1,0:T(8,128)S(1)}, f32[1360,128]{1,0:T(8,128)S(1)}, /*index=5*/f32[1360,128]{1,0:T(8,128)S(1)}) custom-call(s32[32]{0:T(128)S(1)} %concatenate.3.scal, f32[1536,128]{1,0:T(8,128)S(1)} %collective-permute-done.left, ...), custom_call_target="tpu_custom_call" | custom-call | bytes 18000000 | tf_op jit(solution)/shard_map/edge/pallas_call | solution.py:541
  37.5 2.6 %collective-permute-start.4 = (f32[264,128]{1,0:T(8,128)S(1)}, f32[264,128]{1,0:T(8,128)S(1)}, u32[]{:S(2)}, u32[]{:S(2)}) collective-permute-start(f32[264,128]{1,0:T(8,128)S(1)} %get-tuple-element.38), channel_id=1, source_target_pairs={{0,192},{32,224},{64,128},{96,160},{128,64},{160,96},{192,0},{224,... | collective-permute-start | bytes 405512 | tf_op jit(solution)/shard_map/ppermute | solution.py:492
  40.0 0.5 collective-permute-start.3
  40.5 0.3 collective-permute-start.2
  40.8 6.5 %flux.1.part = f32[8,128]{1,0:T(8,128)S(1)} custom-call(f32[2,8,160,128]{3,2,1,0:T(8,128)S(1)} %get-tuple-element.39.se, f32[8,768,128]{2,1,0:T(8,128)S(1)} %get-tuple-element.40.si, f32[1024,128]{1,0:T(8,128)S(1)} %bitcast.20, f32[1360,128]{1,0:T(8,128)S(1)} %get-tuple-element.30.fxi, f32[1360,128]{1,0:T(8,128)S(1)} %get-tuple-element.31.fyi, ...), custom_call_target="tpu_custom_call" | custom-call | bytes 18000000 | tf_op jit(solution)/shard_map/flux/pallas_call | solution.py:556
  47.3 0.0 collective-permute-done.4
  47.3 0.0 collective-permute-done.3
  47.3 0.0 collective-permute-done.2
  47.4 2.2 %collective-permute-start.5 = (f32[4,264,128]{2,1,0:T(8,128)S(1)}, f32[4,264,128]{2,1,0:T(8,128)S(1)}, u32[]{:S(2)}, u32[]{:S(2)}) collective-permute-start(f32[4,264,128]{2,1,0:T(8,128)S(1)} %pad_maximum_fusion.near), channel_id=1, source_target_pairs={{0,32},{32,0},{64,96},{96,64},{128,160},{160,128},{192,224},{224,1... | collective-permute-start | bytes 1622024 | tf_op jit(solution)/shard_map/ppermute | solution.py:492
  49.5 1.6 %collective-permute-done.5.far = f32[4,264,128]{2,1,0:T(8,128)S(1)} collective-permute-done((f32[4,264,128]{2,1,0:T(8,128)S(1)}, f32[4,264,128]{2,1,0:T(8,128)S(1)}, u32[]{:S(2)}, u32[]{:S(2)}) %collective-permute-start.5) | collective-permute-done | bytes 540704 | tf_op jit(solution)/shard_map/ppermute | solution.py:492
  51.1 1.5 %couple.1 = f32[32,8,128]{2,1,0:T(8,128)S(1)} custom-call(s32[32]{0:T(128)S(1)} %concatenate.3.scal, f32[32,1024]{1,0:T(8,128)S(1)} %get-tuple-element.37.window, f32[4,264,128]{2,1,0:T(8,128)S(1)} %pad_maximum_fusion.near, f32[4,264,128]{2,1,0:T(8,128)S(1)} %collective-permute-done.5.far, f32[8,128]{1,0:T(8,128)S(1)} %flux.1.part), custom_call_target="tpu_custom_call" | custom-call | bytes 3000000 | tf_op jit(solution)/shard_map/couple/pallas_call | solution.py:569
  52.6 16.9 %all_to_all.5.got = f32[32,8,128]{2,1,0:T(8,128)S(1)} all-to-all(f32[32,8,128]{2,1,0:T(8,128)S(1)} %couple.1), channel_id=1, replica_groups=mesh['subdomai'=8,'inner'=32] {'inner'}, dimensions={0} | all-to-all | bytes 262144 | tf_op jit(solution)/shard_map/all_to_all | solution.py:579
  69.5 5.0 %finish.1 = (f32[8,1024,128]{2,1,0:T(8,128)}, f32[8,8]{1,0:T(8,128)}, f32[6,8,8]{2,1,0:T(8,128)}) custom-call(s32[32]{0:T(128)S(1)} %concatenate.3.scal, f32[32,8,128]{2,1,0:T(8,128)S(1)} %all_to_all.5.got, f32[8,768,128]{2,1,0:T(8,128)S(1)} %get-tuple-element.40.si, f32[2,8,160,128]{3,2,1,0:T(8,128)S(1)} %get-tuple-element.39.se), custom_call_target="tpu_custom_call" | custom-call | bytes 15000000 | tf_op jit(solution)/shard_map/finish/pallas_call | solution.py:580
  (4 shorter events, 0.0 us)
Async XLA Ops:
  0.6 12.0 %copy-start.1 = (f32[16,64,128]{2,1,0:T(8,128)S(1)}, f32[16,64,128]{2,1,0:T(8,128)}, u32[]{:S(2)}) copy-start(f32[16,64,128]{2,1,0:T(8,128)} %param.8) | copy-start | bytes 1572868
  0.6 12.0 %copy-start.2 = (f32[16,64,128]{2,1,0:T(8,128)S(1)}, f32[16,64,128]{2,1,0:T(8,128)}, u32[]{:S(2)}) copy-start(f32[16,64,128]{2,1,0:T(8,128)} %param.7) | copy-start | bytes 1572868
  0.7 11.9 %copy-start.5 = (s32[1,6]{1,0:T(1,128)S(1)}, s32[1,6]{1,0:T(1,128)}, u32[]{:S(2)}) copy-start(s32[1,6]{1,0:T(1,128)} %param.11) | copy-start | bytes 76
  0.7 11.9 %copy-start.4 = (s32[1,6]{1,0:T(1,128)S(1)}, s32[1,6]{1,0:T(1,128)}, u32[]{:S(2)}) copy-start(s32[1,6]{1,0:T(1,128)} %param.10) | copy-start | bytes 76
  0.7 11.9 %copy-start.3 = (s32[1,2]{1,0:T(1,128)S(1)}, s32[1,2]{1,0:T(1,128)}, u32[]{:S(2)}) copy-start(s32[1,2]{1,0:T(1,128)} %param.9) | copy-start | bytes 28
  3.5 26.4 %collective-permute-start = (f32[1536,128]{1,0:T(8,128)}, f32[1536,128]{1,0:T(8,128)S(1)}, u32[]{:S(2)}, u32[]{:S(2)}) collective-permute-start(f32[1536,128]{1,0:T(8,128)} %get-tuple-element.27), channel_id=1, source_target_pairs={{0,1},{1,2},{2,3},{3,4},{4,5},{5,6},{6,7},{7,8},{8,9},{9,10},{10,1... | collective-permute-start | bytes 2359304 | tf_op jit(solution)/shard_map/ppermute | solution.py:524
  5.7 24.2 %collective-permute-start.1 = (f32[1536,128]{1,0:T(8,128)}, f32[1536,128]{1,0:T(8,128)S(1)}, u32[]{:S(2)}, u32[]{:S(2)}) collective-permute-start(f32[1536,128]{1,0:T(8,128)} %get-tuple-element.28), channel_id=1, source_target_pairs={{0,31},{1,0},{2,1},{3,2},{4,3},{5,4},{6,5},{7,6},{8,7},{9,8},{10,9... | collective-permute-start | bytes 2359304 | tf_op jit(solution)/shard_map/ppermute | solution.py:523
  12.7 2.2 %copy-start = (f32[8,16,64,128]{3,2,1,0:T(8,128)S(1)}, f32[8,16,64,128]{3,2,1,0:T(8,128)}, u32[]{:S(2)}) copy-start(f32[8,16,64,128]{3,2,1,0:T(8,128)} %param.6) | copy-start | bytes 12582916
  37.5 9.9 %collective-permute-start.4 = (f32[264,128]{1,0:T(8,128)S(1)}, f32[264,128]{1,0:T(8,128)S(1)}, u32[]{:S(2)}, u32[]{:S(2)}) collective-permute-start(f32[264,128]{1,0:T(8,128)S(1)} %get-tuple-element.38), channel_id=1, source_target_pairs={{0,192},{32,224},{64,128},{96,160},{128,64},{160,96},{192,0},{224,... | collective-permute-start | bytes 405512 | tf_op jit(solution)/shard_map/ppermute | solution.py:492
  40.0 7.3 %collective-permute-start.3 = (f32[264,128]{1,0:T(8,128)S(1)}, f32[264,128]{1,0:T(8,128)S(1)}, u32[]{:S(2)}, u32[]{:S(2)}) collective-permute-start(f32[264,128]{1,0:T(8,128)S(1)} %get-tuple-element.38), channel_id=1, source_target_pairs={{0,128},{32,160},{64,192},{96,224},{128,0},{160,32},{192,64},{224,... | collective-permute-start | bytes 405512 | tf_op jit(solution)/shard_map/ppermute | solution.py:492
  40.5 6.8 %collective-permute-start.2 = (f32[264,128]{1,0:T(8,128)S(1)}, f32[264,128]{1,0:T(8,128)S(1)}, u32[]{:S(2)}, u32[]{:S(2)}) collective-permute-start(f32[264,128]{1,0:T(8,128)S(1)} %get-tuple-element.38), channel_id=1, source_target_pairs={{0,64},{32,96},{64,0},{96,32},{128,192},{160,224},{192,128},{224,1... | collective-permute-start | bytes 405512 | tf_op jit(solution)/shard_map/ppermute | solution.py:492
  47.4 3.7 %collective-permute-start.5 = (f32[4,264,128]{2,1,0:T(8,128)S(1)}, f32[4,264,128]{2,1,0:T(8,128)S(1)}, u32[]{:S(2)}, u32[]{:S(2)}) collective-permute-start(f32[4,264,128]{2,1,0:T(8,128)S(1)} %pad_maximum_fusion.near), channel_id=1, source_target_pairs={{0,32},{32,0},{64,96},{96,64},{128,160},{160,128},{192,224},{224,1... | collective-permute-start | bytes 1622024 | tf_op jit(solution)/shard_map/ppermute | solution.py:492

commit v3 on v2

--- a/solution.py
+++ b/solution.py
@@ -22,6 +22,7 @@
 PACK = K * HALO + HALO + HALO_ACC
 PAIRS = [(a, b) for b in range(K) for a in range(b + 1)]
 NP = len(PAIRS)
+BY_MATRIX = 4
 HIGHEST = lax.Precision.HIGHEST
 VMEM = pl.BlockSpec(memory_space=pltpu.VMEM)
 SMEM = pl.BlockSpec(memory_space=pltpu.SMEM)
@@ -118,32 +119,58 @@
     rows_loop(lo, hi, step, tiles=tiles)
 
 
-def smooth(scal, src, dst, fx, fy, fz, w, lo, hi, masked, tiles=16, back=0):
+def shifter():
+    row = lax.broadcasted_iota(jnp.int32, (2 * CZ, 2 * CZ), 0) & (CZ - 1)
+    col = lax.broadcasted_iota(jnp.int32, (2 * CZ, 2 * CZ), 1)
+    source = jnp.where(col < CZ, col + 1, col + CZ - 1) & (CZ - 1)
+    return jnp.where(row == source, 1.0, 0.0).astype(F32).astype(jnp.bfloat16)
+
+
+def smooth(scal, src, dst, fx, fy, fz, w, lo, hi, masked, tiles=16, back=0, by_matrix=BY_MATRIX):
     mz = jnp.where(lanes() < scal[1], 1.0 - OMEGA, 0.0).astype(F32)
-
-    def step(r, carry):
-        wt = at(w, r)
-        z = at(fz, r)
-        xp = wt * at(fx, r)
-        xm = wt * at(fx, r - CY)
-        yp = wt * at(fy, r)
-        ym = wt * at(fy, r - 1)
-        zp = wt * z
-        zm = wt * pltpu.roll(z, 1, 1)
-        centre = mz * active(scal, r) if masked else 1.0 - OMEGA
+    shift = shifter()
+
+    def step(i, carry):
+        top = pl.multiple_of(lo + OFF + i * tiles * 8, 8)
+        moved = {}
+        for a in range(by_matrix):
+            v = src[a, pl.ds(top, tiles * 8), :]
+            high = v.astype(jnp.bfloat16)
+            low = (v - high.astype(F32)).astype(jnp.bfloat16)
+            moved[a] = jnp.dot(jnp.concatenate([high, low], axis=1), shift, preferred_element_type=F32)
         stores = []
-        for a in range(K):
-            v = fat(src, a, r)
-            new = (
-                (centre * v + xp * fat(src, a, r + CY))
-                + (xm * fat(src, a, r - CY) + yp * fat(src, a, r + 1))
-                + (ym * fat(src, a, r - 1) + zp * pltpu.roll(v, CZ - 1, 1))
-                + zm * pltpu.roll(v, 1, 1)
-            )
-            stores.append((dst, field_at(a, r - back), new))
-        return stores, carry
-
-    rows_loop(lo, hi, step, tiles=tiles)
+        for j in range(tiles):
+            r = pl.multiple_of(top + j * 8, 8)
+            wt = at(w, r)
+            z = at(fz, r)
+            xp = wt * at(fx, r)
+            xm = wt * at(fx, r - CY)
+            yp = wt * at(fy, r)
+            ym = wt * at(fy, r - 1)
+            zp = wt * z
+            zm = wt * pltpu.roll(z, 1, 1)
+            centre = mz * active(scal, r) if masked else 1.0 - OMEGA
+            for a in range(K):
+                v = fat(src, a, r)
+                if a in moved:
+                    after = moved[a][j * 8 : j * 8 + 8, :CZ]
+                    before = moved[a][j * 8 : j * 8 + 8, CZ:]
+                else:
+                    after = pltpu.roll(v, CZ - 1, 1)
+                    before = pltpu.roll(v, 1, 1)
+                new = (
+                    (centre * v + xp * fat(src, a, r + CY))
+                    + (xm * fat(src, a, r - CY) + yp * fat(src, a, r + 1))
+                    + (ym * fat(src, a, r - 1) + zp * after)
+                    + zm * before
+                )
+                stores.append((dst, field_at(a, r - back), new))
+        for ref, place, value in stores:
+            ref[place] = value
+        return carry
+
+    assert (hi - lo) % (8 * tiles) == 0
+    lax.fori_loop(0, (hi - lo) // (8 * tiles), step, 0)
 
 
 def gram_sums(s, lo, hi, acc, back=0):
@@ -229,8 +256,7 @@
 def pack_kernel(sv, perm, acc, down, up, sem):
     pairs = []
     for out, lo, acc_lo in ((down, 0, 0), (up, SLAB - HALO, SLAB - HALO_ACC)):
-        for a in range(K):
-            pairs.append((sv.at[a, pl.ds(lo, HALO)], out.at[pl.ds(a * HALO, HALO)]))
+        pairs.append((sv.at[:, pl.ds(lo, HALO)], out.at[pl.ds(0, K * HALO)].reshape(K, HALO, CZ)))
         pairs.append((perm.at[pl.ds(lo, HALO)], out.at[pl.ds(K * HALO, HALO)]))
         pairs.append((acc.at[pl.ds(acc_lo, HALO_ACC)], out.at[pl.ds((K + 1) * HALO, HALO_ACC)]))
     wait_all(copy_all(pairs, sem))
@@ -243,23 +269,44 @@
 
 
 BACK = OFF + 2 * CY
+OWN = SLAB - CZ
+EDGE_BACK = (OFF - 32, OFF + OWN)
+
+
+def copy_rows(moves, count, group):
+    def one(i, carry):
+        values = []
+        for j in range(group):
+            for dst, at_dst, src, at_src in moves:
+                rows = [pl.ds(pl.multiple_of(r + (i * group + j) * 8, 8), 8) for r in (at_dst, at_src)]
+                if len(dst.shape) == 2:
+                    values.append((dst, (rows[0], slice(None)), src[rows[1], :]))
+                else:
+                    for a in range(K):
+                        values.append((dst, (a, rows[0], slice(None)), src[a, rows[1], :]))
+        for dst, place, value in values:
+            dst[place] = value
+        return carry
+
+    assert count % (8 * group) == 0
+    lax.fori_loop(0, count // (8 * group), one, 0)
 
 
 def interior_kernel(
-    scal, sv, perm, acc, si, ve, fx, fy, fz, w, gram, first, window, v0, v1, kp, ac, tile, ptile, sem
+    scal, sv, perm, acc, si, ve, kp, ac, fx, fy, fz, w, gram, flux, first, window, v0, v1, tile, ptile, sem
 ):
     slab = pl.ds(OFF, SLAB)
     a, b, c = copy_all([(perm, kp.at[slab]), (acc, ac.at[slab]), (sv, v0.at[:, slab])], sem)
     a.wait()
-    faces(scal, kp, fx, fy, fz, 0, SLAB - CY)
+    faces(scal, kp, fx, fy, fz, 0, SLAB - CY, 20)
     b.wait()
-    weights(ac, fx, fy, fz, w, CY, SLAB - CY)
+    weights(ac, fx, fy, fz, w, CY, SLAB - CY, 16)
     c.wait()
     smooth(scal, v0, v1, fx, fy, fz, w, CY, SLAB - CY, True)
     out = copy_all(
         [
             (v0.at[:, pl.ds(OFF, CZ)], ve.at[0]),
-            (v0.at[:, pl.ds(OFF + SLAB - CZ, CZ)], ve.at[1]),
+            (v0.at[:, pl.ds(OFF + OWN, CZ)], ve.at[1]),
             (v1.at[:, pl.ds(OFF + CY, CZ)], ve.at[2]),
             (v1.at[:, pl.ds(OFF + SLAB - CY - CZ, CZ)], ve.at[3]),
         ],
@@ -269,88 +316,61 @@
     zero = [jnp.zeros((8, CZ), F32)] * NP
     for i, t in enumerate(gram_sums(si, 2 * CY, SLAB - 2 * CY, zero, back=BACK)):
         gram[i] = t
+    for i, t in enumerate(flux_sums(si, ac, fx, fy, fz, 3 * CY, SLAB - 3 * CY, zero, back=BACK)):
+        flux[i] = t
     turned(scal, si, kp, first, window, tile, ptile, (1, 7), back=BACK)
     wait_all(out)
 
 
 def edge_kernel(
-    scal, left, right, perm, acc, ve, fxi, fyi, fzi, wi, gram, firsti, windowi,
-    se, sent, window, fx, fy, fz, v0, v1, s, kp, ac, w, fe, we, tile, ptile, sem,
+    scal, left, right, ve, kpi, aci, fxi, fyi, fzi, wi, gram, firsti, windowi,
+    se, sent, window, fx, fy, fz, v0, v1, kp, ac, w, fe, we, tile, ptile,
 ):
-    pairs = []
-    own = SLAB - CZ
-    for src, lo, acc_lo, near in ((left, -HALO, -HALO_ACC, 0), (right, SLAB, SLAB, own)):
-        pairs.append((src.at[pl.ds(K * HALO, HALO)], kp.at[pl.ds(OFF + lo, HALO)]))
-        pairs.append((src.at[pl.ds((K + 1) * HALO, HALO_ACC)], ac.at[pl.ds(OFF + acc_lo, HALO_ACC)]))
-        pairs.append((perm.at[pl.ds(near, CZ)], kp.at[pl.ds(OFF + near, CZ)]))
-        pairs.append((acc.at[pl.ds(near, CZ)], ac.at[pl.ds(OFF + near, CZ)]))
-    early = len(pairs)
-    for src, lo in ((left, -HALO), (right, SLAB)):
-        for a in range(K):
-            pairs.append((src.at[pl.ds(a * HALO, HALO)], v0.at[a, pl.ds(OFF + lo, HALO)]))
-    for old, new in ((fxi, fx), (fyi, fy), (fzi, fz)):
-        for near, count in ((0, 3 * CY), (SLAB - 4 * CY, 3 * CY)):
-            rows = pl.ds(OFF + near, count)
-            pairs.append((old.at[rows], new.at[rows]))
-    for near in (CY, SLAB - 2 * CY):
-        rows = pl.ds(OFF + near, CY)
-        pairs.append((wi.at[rows], w.at[rows]))
-    pairs.append((ve.at[0], v0.at[:, pl.ds(OFF, CZ)]))
-    pairs.append((ve.at[1], v0.at[:, pl.ds(OFF + own, CZ)]))
-    pairs.append((ve.at[2], v1.at[:, pl.ds(OFF + CY, CZ)]))
-    pairs.append((ve.at[3], v1.at[:, pl.ds(OFF + SLAB - CY - CZ, CZ)]))
-    copies = copy_all(pairs, sem)
-    wait_all(copies[:early])
-    wait_all(copies[early:])
+    ends = ((left, -HALO, -HALO_ACC, 0), (right, SLAB, SLAB, OWN))
+    moves = [(kp, OFF + lo, src, K * HALO) for src, lo, _, _ in ends]
+    copy_rows(moves, HALO, 20)
+    moves = [(ac, OFF + lo, src, (K + 1) * HALO) for src, _, lo, _ in ends]
+    copy_rows(moves, HALO_ACC, 12)
+    copy_rows([(new, OFF + n, old, OFF + n) for new, old in ((kp, kpi), (ac, aci)) for n in (0, OWN)], CZ, 16)
+    both = (0, SLAB - 4 * CY)
+    copy_rows([(new, OFF + n, old, OFF + n) for new, old in ((fx, fxi), (fy, fyi), (fz, fzi)) for n in both], 3 * CY, 8)
+    copy_rows([(w, OFF + n, wi, OFF + n) for n in (CY, SLAB - 2 * CY)], CY, 8)
     faces(scal, kp, fx, fy, fz, -HALO, 0, 20)
     faces(scal, kp, fx, fy, fz, SLAB - CY, SLAB + HALO_ACC, 20)
     weights(ac, fx, fy, fz, w, -HALO_ACC, CY, 20)
     weights(ac, fx, fy, fz, w, SLAB - CY, SLAB + HALO_ACC, 20)
+    for src, lo, _, _ in ends:
+        for a in range(K):
+            copy_rows([(v0.at[a], OFF + lo, src, a * HALO)], HALO, 20)
+    for i, near in enumerate((0, OWN)):
+        copy_rows([(v0, OFF + near, ve.at[i], 0)], CZ, 8)
+    for i, near in enumerate((CY, SLAB - CY - CZ)):
+        copy_rows([(v1, OFF + near, ve.at[2 + i], 0)], CZ, 8)
     smooth(scal, v0, v1, fx, fy, fz, w, -HALO_ACC, CY, True, 20)
     smooth(scal, v0, v1, fx, fy, fz, w, SLAB - CY, SLAB + HALO_ACC, True, 20)
-    smooth(scal, v1, s, fx, fy, fz, w, -32, 2 * CY, False, 20)
-    smooth(scal, v1, s, fx, fy, fz, w, SLAB - 2 * CY, SLAB + 32, False, 20)
-    out = copy_all(
-        [
-            (s.at[:, pl.ds(OFF - 32, EDGE)], se.at[0]),
-            (s.at[:, pl.ds(OFF + own, EDGE)], se.at[1]),
-        ],
-        sem,
-    )
+    smooth(scal, v1, se.at[0], fx, fy, fz, w, -32, 2 * CY, False, 20, EDGE_BACK[0])
+    smooth(scal, v1, se.at[1], fx, fy, fz, w, SLAB - 2 * CY, SLAB + 32, False, 20, EDGE_BACK[1])
     window[:, pl.ds(CZ, INSIDE)] = windowi[...]
     for i in range(INSIDE // CZ):
         sent[pl.ds((i + 1) * FIRST, FIRST), :] = firsti[:, i * CZ : (i + 1) * CZ]
-    for i, lane in ((0, 0), (7, own)):
-        turned(scal, s, kp, fe, we, tile, ptile, (i, i + 1))
+    for i, lane, end in ((0, 0, 0), (7, OWN, 1)):
+        turned(scal, se.at[end], kp, fe, we, tile, ptile, (i, i + 1), EDGE_BACK[end])
         sent[pl.ds(i * FIRST, FIRST), :] = fe[...]
         window[:, pl.ds(lane, CZ)] = we[...]
     acc = [gram[i] for i in range(NP)]
-    acc = gram_sums(s, 0, 2 * CY, acc)
-    acc = gram_sums(s, SLAB - 2 * CY, SLAB, acc)
+    acc = gram_sums(se.at[0], 0, 2 * CY, acc, EDGE_BACK[0])
+    acc = gram_sums(se.at[1], SLAB - 2 * CY, SLAB, acc, EDGE_BACK[1])
     lane = lanes()
     res = jnp.zeros((8, CZ), F32)
     for b, col in enumerate(lane_sums(acc)):
         res = jnp.where(lane == b, col, res)
     sent[pl.ds(SENT - 8, 8), :] = res
-    wait_all(out)
-
-
-def flux_kernel(se, si, acc, fxi, fyi, fzi, fx, fy, fz, part, s, ac, sem):
-    own = SLAB - CZ
-    wait_all(
-        copy_all(
-            [
-                (se.at[0], s.at[:, pl.ds(OFF - 32, EDGE)]),
-                (se.at[1], s.at[:, pl.ds(OFF + own, EDGE)]),
-                (si.at[:, pl.ds(0, CZ)], s.at[:, pl.ds(OFF + CZ, CZ)]),
-                (si.at[:, pl.ds(INSIDE - CZ, CZ)], s.at[:, pl.ds(OFF + own - CZ, CZ)]),
-                (acc, ac.at[pl.ds(OFF, SLAB)]),
-            ],
-            sem,
-        )
-    )
-    acc = [jnp.zeros((8, CZ), F32)] * NP
-    acc = flux_sums(si, ac, fxi, fyi, fzi, 3 * CY, SLAB - 3 * CY, acc, back=BACK)
+
+
+def flux_kernel(se, si, ac, fx, fy, fz, flux, part, s):
+    acc = [flux[i] for i in range(NP)]
+    copy_rows([(s, OFF - 32, se.at[0], 0), (s, OFF + OWN, se.at[1], 0)], EDGE, 4)
+    copy_rows([(s, OFF + CZ, si, 0), (s, OFF + OWN - CZ, si, INSIDE - CZ)], CZ, 4)
     acc = flux_sums(s, ac, fx, fy, fz, 0, CY, acc, before=False)
     acc = flux_sums(s, ac, fx, fy, fz, CY, 3 * CY, acc)
     acc = flux_sums(s, ac, fx, fy, fz, SLAB - 3 * CY, SLAB - CY, acc)
@@ -516,7 +536,7 @@
         out_shape=(shape(PACK, CZ),) * 2,
         in_specs=[HBM] * 3,
         out_specs=(VMEM,) * 2,
-        scratch_shapes=[pltpu.SemaphoreType.DMA((20,))],
+        scratch_shapes=[pltpu.SemaphoreType.DMA((6,))],
         compiler_params=params(60),
         name="pack",
     )(sv, perm, acc)
@@ -525,44 +545,40 @@
     field, plain = pltpu.VMEM((K, RT, CZ), F32), pltpu.VMEM((RT, CZ), F32)
     turning = [pltpu.VMEM((K, CZ, CZ), F32), pltpu.VMEM((CZ, CZ), F32)]
     turn = shape(FIRST, INSIDE)
-    si, ve, fx, fy, fz, w, gram, first, window = pl.pallas_call(
+    si, ve, kp, ac, fx, fy, fz, w, gram, flux, first, window = pl.pallas_call(
         interior_kernel,
         out_shape=(shape(K, INSIDE, CZ), shape(4, K, CZ, CZ))
-        + (shape(RT, CZ),) * 4
-        + (shape(NP, 8, CZ),)
+        + (shape(RT, CZ),) * 6
+        + (shape(NP, 8, CZ),) * 2
         + (turn,) * 2,
         in_specs=[SMEM, HBM, HBM, HBM],
-        out_specs=(VMEM,) * 9,
-        scratch_shapes=[field] * 2 + [plain] * 2 + turning + [pltpu.SemaphoreType.DMA((4,))],
-        compiler_params=params(40),
-        cost_estimate=cost(13),
+        out_specs=(VMEM,) * 12,
+        scratch_shapes=[field] * 2 + turning + [pltpu.SemaphoreType.DMA((4,))],
+        compiler_params=params(36),
+        cost_estimate=cost(15),
         name="interior",
     )(scal, sv, perm, acc)
     se, sent, window, fxe, fye, fze = pl.pallas_call(
         edge_kernel,
         out_shape=(shape(2, K, EDGE, CZ), shape(SENT, CZ), shape(FIRST, SLAB)) + (shape(RT, CZ),) * 3,
-        in_specs=[SMEM] + [VMEM] * 2 + [HBM] * 2 + [VMEM] * 8,
+        in_specs=[SMEM] + [VMEM] * 12,
         out_specs=(VMEM,) * 6,
-        scratch_shapes=[field] * 3
-        + [plain] * 3
-        + [pltpu.VMEM((FIRST, CZ), F32)] * 2
-        + turning
-        + [pltpu.SemaphoreType.DMA((48,))],
+        scratch_shapes=[field] * 2 + [plain] * 3 + [pltpu.VMEM((FIRST, CZ), F32)] * 2 + turning,
         compiler_params=params(24),
         cost_estimate=cost(6),
         name="edge",
-    )(scal, left, right, perm, acc, ve, fx, fy, fz, w, gram, first, window)
+    )(scal, left, right, ve, kp, ac, fx, fy, fz, w, gram, first, window)
     moved = [swap(sent, bits) for bits in (2, 4, 6)]
     part = pl.pallas_call(
         flux_kernel,
         out_shape=shape(8, CZ),
-        in_specs=[VMEM] * 2 + [HBM] + [VMEM] * 6,
+        in_specs=[VMEM] * 7,
         out_specs=VMEM,
-        scratch_shapes=[field, plain, pltpu.SemaphoreType.DMA((5,))],
+        scratch_shapes=[field],
         compiler_params=params(10),
-        cost_estimate=cost(6),
+        cost_estimate=cost(3),
         name="flux",
-    )(se, si, acc, fx, fy, fz, fxe, fye, fze)
+    )(se, si, ac, fxe, fye, fze, flux)
     moved, part = lax.optimization_barrier((moved, part))
     near = jnp.stack([sent] + moved)
     far = swap(near, 1)

time: 75.3 us -> 69.4 us (0.922)
  Pallas kernels: 34.5 us -> 29.3 us
  starting transfers between devices: 14.5 us -> 15.5 us
    pallas_call x1, Pallas kernels: 6.5 us -> 2.43 us  [body(): pl.pallas_call(flux_kernel, out_shape=shape(8, CZ), in_specs=[VMEM] * 7,...]
    pallas_call x1, Pallas kernels: 7.5 us -> 3.52 us  [body(): pl.pallas_call(edge_kernel, out_shape=(shape(2, K, EDGE, CZ), shape(SENT,...]
    ppermute x1, waiting for transfers between devices: 3.97 us -> 0.83 us  [body(): lax.ppermute(up, 'inner', [(i, (i + 1) % groups) for i in range(groups)])]
    pallas_call x1, Pallas kernels: 11.1 us -> 14.2 us  [body(): pl.pallas_call(interior_kernel, out_shape=(shape(K, INSIDE, CZ), shape(4,...]
    ppermute x4, waiting for transfers between devices: 1.57 us -> 4.23 us  [swap(): lax.ppermute(x, 'subdomai', [(i, i ^ bits) for i in range(lax.axis_size('...]
    ppermute x4, starting transfers between devices: 5.5 us -> 6.52 us  [swap(): lax.ppermute(x, 'subdomai', [(i, i ^ bits) for i in range(lax.axis_size('...]
  transfers between devices with their start and end apart: 6 -> 6, of which waited for: 2 -> 5; matrix products, arithmetic and copies ran while one was open for 0% -> 0% of each run, Pallas kernels for 24% -> 24%
where the time goes in v3:
time: 69.4 us; the launch traced here: 69.3 us
  Pallas kernels  29.3 us (42%)
  blocking collectives  16.2 us (23%)
  starting transfers between devices  15.5 us (22%)
  waiting for transfers between devices  5.06 us (7%)
  local copies, waits for them, and re-layouts  2.29 us (3%)
  between operations  0.75 us (1%)
    all_to_all x1, blocking collectives, body(): got = lax.all_to_all(msg, 'inner', 0, 0)  16.2 us
    pallas_call x1, Pallas kernels, body(): pl.pallas_call(interior_kernel, out_shape=(shape(K, INSIDE, CZ), shape(4,...  14.2 us
    ppermute x1, starting transfers between devices, body(): lax.ppermute(down, 'inner', [(i, (i - 1) % groups) for i in range(groups)])  6.82 us
    ppermute x4, starting transfers between devices, swap(): lax.ppermute(x, 'subdomai', [(i, i ^ bits) for i in range(lax.axis_size('...  6.52 us
    pallas_call x1, Pallas kernels, body(): pl.pallas_call(functools.partial(finish_kernel, 1.0 / cells), out_shape=(...  5.01 us
    ppermute x4, waiting for transfers between devices, swap(): lax.ppermute(x, 'subdomai', [(i, i ^ bits) for i in range(lax.axis_size('...  4.23 us
    pallas_call x1, Pallas kernels, body(): pl.pallas_call(edge_kernel, out_shape=(shape(2, K, EDGE, CZ), shape(SENT,...  3.52 us
    pallas_call x1, Pallas kernels, body(): pl.pallas_call(pack_kernel, out_shape=(shape(PACK, CZ),) * 2, in_specs=[H...  2.63 us
  transfers between devices with their start and end apart: 6, of which 5 were waited for; matrix products, arithmetic and copies ran while one was open for 0% of the time, Pallas kernels for 24%

profile of v3, /device:TPU:1, one launch (start us, length us, event | category | flops | bytes accessed | tf_op | source)
XLA Modules:
  0.0 69.3 jit_solution(5388999709932078043)
XLA Ops:
  0.6 0.0 copy-start.2
  0.6 0.0 copy-start.1
  0.7 0.0 copy-start.5
  0.7 0.0 copy-start.4
  0.7 0.0 copy-start.3
  0.7 2.6 %pack.1 = (f32[1536,128]{1,0:T(8,128)}, f32[1536,128]{1,0:T(8,128)}) custom-call(f32[8,1024,128]{2,1,0:T(8,128)} %bitcast.15, f32[1024,128]{1,0:T(8,128)} %bitcast.17, f32[1024,128]{1,0:T(8,128)} %bitcast.19), custom_call_target="tpu_custom_call" | custom-call | tf_op jit(solution)/shard_map/pack/pallas_call | solution.py:534
  3.3 2.2 %collective-permute-start = (f32[1536,128]{1,0:T(8,128)}, f32[1536,128]{1,0:T(8,128)S(1)}, u32[]{:S(2)}, u32[]{:S(2)}) collective-permute-start(f32[1536,128]{1,0:T(8,128)} %get-tuple-element.30), channel_id=1, source_target_pairs={{0,1},{1,2},{2,3},{3,4},{4,5},{5,6},{6,7},{7,8},{8,9},{9,10},{10,1... | collective-permute-start | bytes 2359304 | tf_op jit(solution)/shard_map/ppermute | solution.py:544
  5.5 6.8 %collective-permute-start.1 = (f32[1536,128]{1,0:T(8,128)}, f32[1536,128]{1,0:T(8,128)S(1)}, u32[]{:S(2)}, u32[]{:S(2)}) collective-permute-start(f32[1536,128]{1,0:T(8,128)} %get-tuple-element.31), channel_id=1, source_target_pairs={{0,31},{1,0},{2,1},{3,2},{4,3},{5,4},{6,5},{7,6},{8,7},{9,8},{10,9... | collective-permute-start | bytes 2359304 | tf_op jit(solution)/shard_map/ppermute | solution.py:543
  12.3 0.0 copy-done.5
  12.4 0.0 copy-done.4
  12.4 0.0 copy-done.3
  12.4 0.1 concatenate.3.scal
  12.5 0.0 copy-done.2
  12.5 0.0 copy-done.1
  12.5 0.0 copy-start
  12.5 2.2 %copy-done = f32[8,16,64,128]{3,2,1,0:T(8,128)S(1)} copy-done((f32[8,16,64,128]{3,2,1,0:T(8,128)S(1)}, f32[8,16,64,128]{3,2,1,0:T(8,128)}, u32[]{:S(2)}) %copy-start) | copy-done | bytes 4194328
  14.7 14.2 %interior.1 = (f32[8,768,128]{2,1,0:T(8,128)S(1)}, f32[4,8,128,128]{3,2,1,0:T(8,128)S(1)}, f32[1360,128]{1,0:T(8,128)S(1)}, f32[1360,128]{1,0:T(8,128)S(1)}, f32...) custom-call(s32[32]{0:T(128)S(1)} %concatenate.3.scal, ...), custom_call_target="tpu_custom_call" | custom-call | bytes 45000000 | tf_op jit(solution)/shard_map/interior/pallas_call | solution.py:548
  28.9 0.8 %collective-permute-done.left = f32[1536,128]{1,0:T(8,128)S(1)} collective-permute-done((f32[1536,128]{1,0:T(8,128)}, f32[1536,128]{1,0:T(8,128)S(1)}, u32[]{:S(2)}, u32[]{:S(2)}) %collective-permute-start) | collective-permute-done | bytes 786464 | tf_op jit(solution)/shard_map/ppermute | solution.py:544
  29.7 0.0 collective-permute-done.1.right
  29.7 3.5 %edge.1 = (f32[2,8,160,128]{3,2,1,0:T(8,128)S(1)}, f32[264,128]{1,0:T(8,128)S(1)}, f32[32,1024]{1,0:T(8,128)S(1)}, f32[1360,128]{1,0:T(8,128)S(1)}, f32[1360,128]{1,0:T(8,128)S(1)}, /*index=5*/f32[1360,128]{1,0:T(8,128)S(1)}) custom-call(s32[32]{0:T(128)S(1)} %concatenate.3.scal, f32[1536,128]{1,0:T(8,128)S(1)} %collective-permute-done.left, ...), custom_call_target="tpu_custom_call" | custom-call | bytes 18000000 | tf_op jit(solution)/shard_map/edge/pallas_call | solution.py:561
  33.2 2.5 %collective-permute-start.4 = (f32[264,128]{1,0:T(8,128)S(1)}, f32[264,128]{1,0:T(8,128)S(1)}, u32[]{:S(2)}, u32[]{:S(2)}) collective-permute-start(f32[264,128]{1,0:T(8,128)S(1)} %get-tuple-element.43), channel_id=1, source_target_pairs={{0,192},{32,224},{64,128},{96,160},{128,64},{160,96},{192,0},{224,... | collective-permute-start | bytes 405512 | tf_op jit(solution)/shard_map/ppermute | solution.py:512
  35.8 0.5 collective-permute-start.3
  36.3 0.3 collective-permute-start.2
  36.6 2.4 %flux.1.part = f32[8,128]{1,0:T(8,128)S(1)} custom-call(f32[2,8,160,128]{3,2,1,0:T(8,128)S(1)} %get-tuple-element.44.se, f32[8,768,128]{2,1,0:T(8,128)S(1)} %get-tuple-element.45.si, f32[1360,128]{1,0:T(8,128)S(1)} %get-tuple-element.34.aci.ac, f32[1360,128]{1,0:T(8,128)S(1)} %get-tuple-element.46.fx, f32[1360,128]{1,0:T(8,128)S(1)} %get-tuple-element.47.fy, ...), custom_call_target="tpu_custom_call" | custom-call | bytes 9000000 | tf_op jit(solution)/shard_map/flux/pallas_call | solution.py:572
  39.0 1.6 %collective-permute-done.4 = f32[264,128]{1,0:T(8,128)S(1)} collective-permute-done((f32[264,128]{1,0:T(8,128)S(1)}, f32[264,128]{1,0:T(8,128)S(1)}, u32[]{:S(2)}, u32[]{:S(2)}) %collective-permute-start.4) | collective-permute-done | bytes 135200 | tf_op jit(solution)/shard_map/ppermute | solution.py:512
  40.6 0.6 collective-permute-done.3
  41.3 0.4 collective-permute-done.2
  41.7 3.2 %collective-permute-start.5 = (f32[4,264,128]{2,1,0:T(8,128)S(1)}, f32[4,264,128]{2,1,0:T(8,128)S(1)}, u32[]{:S(2)}, u32[]{:S(2)}) collective-permute-start(f32[4,264,128]{2,1,0:T(8,128)S(1)} %pad_maximum_fusion.near), channel_id=1, source_target_pairs={{0,32},{32,0},{64,96},{96,64},{128,160},{160,128},{192,224},{224,1... | collective-permute-start | bytes 1622024 | tf_op jit(solution)/shard_map/ppermute | solution.py:512
  44.9 1.6 %collective-permute-done.5.far = f32[4,264,128]{2,1,0:T(8,128)S(1)} collective-permute-done((f32[4,264,128]{2,1,0:T(8,128)S(1)}, f32[4,264,128]{2,1,0:T(8,128)S(1)}, u32[]{:S(2)}, u32[]{:S(2)}) %collective-permute-start.5) | collective-permute-done | bytes 540704 | tf_op jit(solution)/shard_map/ppermute | solution.py:512
  46.5 1.5 %couple.1 = f32[32,8,128]{2,1,0:T(8,128)S(1)} custom-call(s32[32]{0:T(128)S(1)} %concatenate.3.scal, f32[32,1024]{1,0:T(8,128)S(1)} %get-tuple-element.42.window, f32[4,264,128]{2,1,0:T(8,128)S(1)} %pad_maximum_fusion.near, f32[4,264,128]{2,1,0:T(8,128)S(1)} %collective-permute-done.5.far, f32[8,128]{1,0:T(8,128)S(1)} %flux.1.part), custom_call_target="tpu_custom_call" | custom-call | bytes 3000000 | tf_op jit(solution)/shard_map/couple/pallas_call | solution.py:585
  48.0 16.2 %all_to_all.5.got = f32[32,8,128]{2,1,0:T(8,128)S(1)} all-to-all(f32[32,8,128]{2,1,0:T(8,128)S(1)} %couple.1), channel_id=1, replica_groups=mesh['subdomai'=8,'inner'=32] {'inner'}, dimensions={0} | all-to-all | bytes 262144 | tf_op jit(solution)/shard_map/all_to_all | solution.py:595
  64.3 5.0 %finish.1 = (f32[8,1024,128]{2,1,0:T(8,128)}, f32[8,8]{1,0:T(8,128)}, f32[6,8,8]{2,1,0:T(8,128)}) custom-call(s32[32]{0:T(128)S(1)} %concatenate.3.scal, f32[32,8,128]{2,1,0:T(8,128)S(1)} %all_to_all.5.got, f32[8,768,128]{2,1,0:T(8,128)S(1)} %get-tuple-element.45.si, f32[2,8,160,128]{3,2,1,0:T(8,128)S(1)} %get-tuple-element.44.se), custom_call_target="tpu_custom_call" | custom-call | bytes 15000000 | tf_op jit(solution)/shard_map/finish/pallas_call | solution.py:596
  (4 shorter events, 0.0 us)
Async XLA Ops:
  0.6 11.8 %copy-start.2 = (f32[16,64,128]{2,1,0:T(8,128)S(1)}, f32[16,64,128]{2,1,0:T(8,128)}, u32[]{:S(2)}) copy-start(f32[16,64,128]{2,1,0:T(8,128)} %param.8) | copy-start | bytes 1572868
  0.6 11.8 %copy-start.1 = (f32[16,64,128]{2,1,0:T(8,128)S(1)}, f32[16,64,128]{2,1,0:T(8,128)}, u32[]{:S(2)}) copy-start(f32[16,64,128]{2,1,0:T(8,128)} %param.7) | copy-start | bytes 1572868
  0.7 11.7 %copy-start.5 = (s32[1,6]{1,0:T(1,128)S(1)}, s32[1,6]{1,0:T(1,128)}, u32[]{:S(2)}) copy-start(s32[1,6]{1,0:T(1,128)} %param.11) | copy-start | bytes 76
  0.7 11.7 %copy-start.4 = (s32[1,6]{1,0:T(1,128)S(1)}, s32[1,6]{1,0:T(1,128)}, u32[]{:S(2)}) copy-start(s32[1,6]{1,0:T(1,128)} %param.10) | copy-start | bytes 76
  0.7 11.7 %copy-start.3 = (s32[1,2]{1,0:T(1,128)S(1)}, s32[1,2]{1,0:T(1,128)}, u32[]{:S(2)}) copy-start(s32[1,2]{1,0:T(1,128)} %param.9) | copy-start | bytes 28
  3.3 26.4 %collective-permute-start = (f32[1536,128]{1,0:T(8,128)}, f32[1536,128]{1,0:T(8,128)S(1)}, u32[]{:S(2)}, u32[]{:S(2)}) collective-permute-start(f32[1536,128]{1,0:T(8,128)} %get-tuple-element.30), channel_id=1, source_target_pairs={{0,1},{1,2},{2,3},{3,4},{4,5},{5,6},{6,7},{7,8},{8,9},{9,10},{10,1... | collective-permute-start | bytes 2359304 | tf_op jit(solution)/shard_map/ppermute | solution.py:544
  5.5 24.2 %collective-permute-start.1 = (f32[1536,128]{1,0:T(8,128)}, f32[1536,128]{1,0:T(8,128)S(1)}, u32[]{:S(2)}, u32[]{:S(2)}) collective-permute-start(f32[1536,128]{1,0:T(8,128)} %get-tuple-element.31), channel_id=1, source_target_pairs={{0,31},{1,0},{2,1},{3,2},{4,3},{5,4},{6,5},{7,6},{8,7},{9,8},{10,9... | collective-permute-start | bytes 2359304 | tf_op jit(solution)/shard_map/ppermute | solution.py:543
  12.5 2.2 %copy-start = (f32[8,16,64,128]{3,2,1,0:T(8,128)S(1)}, f32[8,16,64,128]{3,2,1,0:T(8,128)}, u32[]{:S(2)}) copy-start(f32[8,16,64,128]{3,2,1,0:T(8,128)} %param.6) | copy-start | bytes 12582916
  33.2 7.4 %collective-permute-start.4 = (f32[264,128]{1,0:T(8,128)S(1)}, f32[264,128]{1,0:T(8,128)S(1)}, u32[]{:S(2)}, u32[]{:S(2)}) collective-permute-start(f32[264,128]{1,0:T(8,128)S(1)} %get-tuple-element.43), channel_id=1, source_target_pairs={{0,192},{32,224},{64,128},{96,160},{128,64},{160,96},{192,0},{224,... | collective-permute-start | bytes 405512 | tf_op jit(solution)/shard_map/ppermute | solution.py:512
  35.8 5.5 %collective-permute-start.3 = (f32[264,128]{1,0:T(8,128)S(1)}, f32[264,128]{1,0:T(8,128)S(1)}, u32[]{:S(2)}, u32[]{:S(2)}) collective-permute-start(f32[264,128]{1,0:T(8,128)S(1)} %get-tuple-element.43), channel_id=1, source_target_pairs={{0,128},{32,160},{64,192},{96,224},{128,0},{160,32},{192,64},{224,... | collective-permute-start | bytes 405512 | tf_op jit(solution)/shard_map/ppermute | solution.py:512
  36.3 5.4 %collective-permute-start.2 = (f32[264,128]{1,0:T(8,128)S(1)}, f32[264,128]{1,0:T(8,128)S(1)}, u32[]{:S(2)}, u32[]{:S(2)}) collective-permute-start(f32[264,128]{1,0:T(8,128)S(1)} %get-tuple-element.43), channel_id=1, source_target_pairs={{0,64},{32,96},{64,0},{96,32},{128,192},{160,224},{192,128},{224,1... | collective-permute-start | bytes 405512 | tf_op jit(solution)/shard_map/ppermute | solution.py:512
  41.7 4.8 %collective-permute-start.5 = (f32[4,264,128]{2,1,0:T(8,128)S(1)}, f32[4,264,128]{2,1,0:T(8,128)S(1)}, u32[]{:S(2)}, u32[]{:S(2)}) collective-permute-start(f32[4,264,128]{2,1,0:T(8,128)S(1)} %pad_maximum_fusion.near), channel_id=1, source_target_pairs={{0,32},{32,0},{64,96},{96,64},{128,160},{160,128},{192,224},{224,1... | collective-permute-start | bytes 1622024 | tf_op jit(solution)/shard_map/ppermute | solution.py:512

commit v4 on v3

--- a/solution.py
+++ b/solution.py
@@ -34,18 +34,26 @@
     return jax.ShapeDtypeStruct(dims, F32)
 
 
+def aligned(x, n):
+    return x if isinstance(x, int) else pl.multiple_of(x, n)
+
+
+def loop(lo, hi, step, init):
+    return step(lo, init) if hi - lo == 1 else lax.fori_loop(lo, hi, step, init)
+
+
 def rows_loop(lo, hi, step, init=(), tiles=4):
     def one(i, carry):
         stores = []
         for j in range(tiles):
-            more, carry = step(pl.multiple_of(lo + OFF + (i * tiles + j) * 8, 8), carry)
+            more, carry = step(aligned(lo + OFF + (i * tiles + j) * 8, 8), carry)
             stores += more
         for ref, place, value in stores:
             ref[place] = value
         return carry
 
     assert (hi - lo) % (8 * tiles) == 0
-    return lax.fori_loop(0, (hi - lo) // (8 * tiles), one, init)
+    return loop(0, (hi - lo) // (8 * tiles), one, init)
 
 
 def tile_at(row):
@@ -73,7 +81,7 @@
 
 
 def layer_of(row):
-    return lax.shift_right_arithmetic(row + (192 - OFF), 6) - 3
+    return ((row + (192 - OFF)) >> 6) - 3
 
 
 def active(scal, row, more=0):
@@ -119,6 +127,11 @@
     rows_loop(lo, hi, step, tiles=tiles)
 
 
+def pieces(v):
+    high = v.astype(jnp.bfloat16)
+    return high, (v - high.astype(F32)).astype(jnp.bfloat16)
+
+
 def shifter():
     row = lax.broadcasted_iota(jnp.int32, (2 * CZ, 2 * CZ), 0) & (CZ - 1)
     col = lax.broadcasted_iota(jnp.int32, (2 * CZ, 2 * CZ), 1)
@@ -131,16 +144,14 @@
     shift = shifter()
 
     def step(i, carry):
-        top = pl.multiple_of(lo + OFF + i * tiles * 8, 8)
+        top = aligned(lo + OFF + i * tiles * 8, 8)
         moved = {}
         for a in range(by_matrix):
             v = src[a, pl.ds(top, tiles * 8), :]
-            high = v.astype(jnp.bfloat16)
-            low = (v - high.astype(F32)).astype(jnp.bfloat16)
-            moved[a] = jnp.dot(jnp.concatenate([high, low], axis=1), shift, preferred_element_type=F32)
+            moved[a] = jnp.dot(jnp.concatenate(pieces(v), axis=1), shift, preferred_element_type=F32)
         stores = []
         for j in range(tiles):
-            r = pl.multiple_of(top + j * 8, 8)
+            r = aligned(top + j * 8, 8)
             wt = at(w, r)
             z = at(fz, r)
             xp = wt * at(fx, r)
@@ -170,7 +181,7 @@
         return carry
 
     assert (hi - lo) % (8 * tiles) == 0
-    lax.fori_loop(0, (hi - lo) // (8 * tiles), step, 0)
+    loop(0, (hi - lo) // (8 * tiles), step, 0)
 
 
 def gram_sums(s, lo, hi, acc, back=0):
@@ -178,7 +189,7 @@
         v = [fat(s, a, r - back) for a in range(K)]
         return [], tuple(t + v[a] * v[b] for t, (a, b) in zip(acc, PAIRS))
 
-    return rows_loop(lo, hi, step, tuple(acc), tiles=4)
+    return rows_loop(lo, hi, step, tuple(acc), tiles=8)
 
 
 def flux_sums(s, ac, fx, fy, fz, lo, hi, acc, before=True, after=True, back=0):
@@ -226,7 +237,7 @@
         ptile[...] = kp[pl.ds(row, CZ), :].T
         kw = ptile[pl.ds(start, WMAX), :]
         for a in range(K):
-            tile[a] = s[a, pl.ds(pl.multiple_of(row - back, 8), CZ), :].T
+            tile[a] = s[a, pl.ds(aligned(row - back, 8), CZ), :].T
         for a in range(K):
             u = tile[a, pl.ds(start, WMAX), :] * kw
             f = tile[a, pl.ds(0, WMAX), :]
@@ -235,10 +246,10 @@
                 window[pl.ds(t * K + a, 1), pl.ds(lane, CZ)] = u[t : t + 1]
 
     def one(block, carry):
-        step(block, pl.multiple_of(OFF + block * CZ, 8), pl.multiple_of((block - blocks[0]) * CZ, CZ))
+        step(block, aligned(OFF + block * CZ, 8), aligned((block - blocks[0]) * CZ, CZ))
         return carry
 
-    lax.fori_loop(blocks[0], blocks[1], one, 0)
+    loop(blocks[0], blocks[1], one, 0)
 
 
 def copy_all(pairs, sem):
@@ -278,7 +289,7 @@
         values = []
         for j in range(group):
             for dst, at_dst, src, at_src in moves:
-                rows = [pl.ds(pl.multiple_of(r + (i * group + j) * 8, 8), 8) for r in (at_dst, at_src)]
+                rows = [pl.ds(aligned(r + (i * group + j) * 8, 8), 8) for r in (at_dst, at_src)]
                 if len(dst.shape) == 2:
                     values.append((dst, (rows[0], slice(None)), src[rows[1], :]))
                 else:
@@ -289,7 +300,7 @@
         return carry
 
     assert count % (8 * group) == 0
-    lax.fori_loop(0, count // (8 * group), one, 0)
+    loop(0, count // (8 * group), one, 0)
 
 
 def interior_kernel(
@@ -411,9 +422,13 @@
                 rows = pl.ds(i * FIRST + t * K, K)
                 value = jnp.where(odd, far[place, rows, :], near[place, rows, :])
                 chosen[pl.ds((t * NB + n) * K, K), i * CZ : (i + 1) * CZ] = value
-    prod[:, : WMAX * NB * K] = lax.dot_general(
-        window[...], chosen[...], (((1,), (1,)), ((), ())), precision=HIGHEST, preferred_element_type=F32
-    )
+    mine, mine_low = pieces(window[...])
+    theirs, theirs_low = pieces(chosen[...])
+    both = (((1,), (1,)), ((), ()))
+    prod[:, : WMAX * NB * K] = (
+        lax.dot_general(mine, theirs_low, both, preferred_element_type=F32)
+        + lax.dot_general(mine_low, theirs, both, preferred_element_type=F32)
+    ) + lax.dot_general(mine, theirs, both, preferred_element_type=F32)
     lane = lax.broadcasted_iota(jnp.int32, (8, 2 * CZ), 1)
     total = jnp.zeros((8, 2 * CZ), F32)
     for t in range(WMAX):
@@ -469,8 +484,8 @@
 
         def step(j, carry, src=src, i=i):
             stores = []
-            for t in range(4):
-                r = pl.multiple_of(j * 32 + t * 8, 8)
+            for t in range(8):
+                r = pl.multiple_of(j * 64 + t * 8, 8)
                 v = [src[a, pl.ds(r, 8), :] for a in range(K)]
                 for a in range(K):
                     x = c[0, a] * v[0]
@@ -481,7 +496,7 @@
                 out[i, a, pl.ds(r, 8), :] = x
             return carry
 
-        lax.fori_loop(0, CZ // 32, step, 0)
+        lax.fori_loop(0, CZ // 64, step, 0)
         copies.append(pltpu.make_async_copy(out.at[i], basis.at[:, pl.ds(i * CZ, CZ)], sem.at[i]))
         copies[-1].start()
     others = eliminate([pltpu.roll(total, CZ - OTHERS - m * K, 1) for m in range(SUBDOMAINS - 1)])

time: 69.4 us -> 68.9 us (level)
  no operation moved by 1% of the time
where the time goes in v4:
time: 68.9 us; the launch traced here: 68.7 us
  Pallas kernels  28.7 us (42%)
  blocking collectives  16.2 us (24%)
  starting transfers between devices  15.6 us (23%)
  waiting for transfers between devices  5.2 us (8%)
  local copies, waits for them, and re-layouts  2.29 us (3%)
  between operations  0.75 us (1%)
    all_to_all x1, blocking collectives, body(): got = lax.all_to_all(msg, 'inner', 0, 0)  16.2 us
    pallas_call x1, Pallas kernels, body(): pl.pallas_call(interior_kernel, out_shape=(shape(K, INSIDE, CZ), shape(4,...  14.1 us
    ppermute x1, starting transfers between devices, body(): lax.ppermute(down, 'inner', [(i, (i - 1) % groups) for i in range(groups)])  6.82 us
    ppermute x4, starting transfers between devices, swap(): lax.ppermute(x, 'subdomai', [(i, i ^ bits) for i in range(lax.axis_size('...  6.54 us
    pallas_call x1, Pallas kernels, body(): pl.pallas_call(functools.partial(finish_kernel, 1.0 / cells), out_shape=(...  4.91 us
    ppermute x4, waiting for transfers between devices, swap(): lax.ppermute(x, 'subdomai', [(i, i ^ bits) for i in range(lax.axis_size('...  4.22 us
    pallas_call x1, Pallas kernels, body(): pl.pallas_call(edge_kernel, out_shape=(shape(2, K, EDGE, CZ), shape(SENT,...  3.44 us
    pallas_call x1, Pallas kernels, body(): pl.pallas_call(pack_kernel, out_shape=(shape(PACK, CZ),) * 2, in_specs=[H...  2.63 us
  transfers between devices with their start and end apart: 6, of which 5 were waited for; matrix products, arithmetic and copies ran while one was open for 0% of the time, Pallas kernels for 24%

profile of v4, /device:TPU:1, one launch (start us, length us, event | category | flops | bytes accessed | tf_op | source)
XLA Modules:
  0.0 68.7 jit_solution(5272003931503450143)
XLA Ops:
  0.6 0.0 copy-start.2
  0.6 0.0 copy-start.1
  0.7 0.0 copy-start.5
  0.7 0.0 copy-start.4
  0.7 0.0 copy-start.3
  0.7 2.6 %pack.1 = (f32[1536,128]{1,0:T(8,128)}, f32[1536,128]{1,0:T(8,128)}) custom-call(f32[8,1024,128]{2,1,0:T(8,128)} %bitcast.15, f32[1024,128]{1,0:T(8,128)} %bitcast.17, f32[1024,128]{1,0:T(8,128)} %bitcast.19), custom_call_target="tpu_custom_call" | custom-call | tf_op jit(solution)/shard_map/pack/pallas_call | solution.py:549
  3.3 2.2 %collective-permute-start = (f32[1536,128]{1,0:T(8,128)}, f32[1536,128]{1,0:T(8,128)S(1)}, u32[]{:S(2)}, u32[]{:S(2)}) collective-permute-start(f32[1536,128]{1,0:T(8,128)} %get-tuple-element.30), channel_id=1, source_target_pairs={{0,1},{1,2},{2,3},{3,4},{4,5},{5,6},{6,7},{7,8},{8,9},{9,10},{10,1... | collective-permute-start | bytes 2359304 | tf_op jit(solution)/shard_map/ppermute | solution.py:559
  5.5 6.8 %collective-permute-start.1 = (f32[1536,128]{1,0:T(8,128)}, f32[1536,128]{1,0:T(8,128)S(1)}, u32[]{:S(2)}, u32[]{:S(2)}) collective-permute-start(f32[1536,128]{1,0:T(8,128)} %get-tuple-element.31), channel_id=1, source_target_pairs={{0,31},{1,0},{2,1},{3,2},{4,3},{5,4},{6,5},{7,6},{8,7},{9,8},{10,9... | collective-permute-start | bytes 2359304 | tf_op jit(solution)/shard_map/ppermute | solution.py:558
  12.3 0.0 copy-done.5
  12.4 0.0 copy-done.4
  12.4 0.0 copy-done.3
  12.4 0.1 concatenate.3.scal
  12.5 0.0 copy-done.2
  12.5 0.0 copy-done.1
  12.5 0.0 copy-start
  12.5 2.2 %copy-done = f32[8,16,64,128]{3,2,1,0:T(8,128)S(1)} copy-done((f32[8,16,64,128]{3,2,1,0:T(8,128)S(1)}, f32[8,16,64,128]{3,2,1,0:T(8,128)}, u32[]{:S(2)}) %copy-start) | copy-done | bytes 4194328
  14.7 14.1 %interior.1 = (f32[8,768,128]{2,1,0:T(8,128)S(1)}, f32[4,8,128,128]{3,2,1,0:T(8,128)S(1)}, f32[1360,128]{1,0:T(8,128)S(1)}, f32[1360,128]{1,0:T(8,128)S(1)}, f32...) custom-call(s32[32]{0:T(128)S(1)} %concatenate.3.scal, ...), custom_call_target="tpu_custom_call" | custom-call | bytes 45000000 | tf_op jit(solution)/shard_map/interior/pallas_call | solution.py:563
  28.7 1.0 %collective-permute-done.left = f32[1536,128]{1,0:T(8,128)S(1)} collective-permute-done((f32[1536,128]{1,0:T(8,128)}, f32[1536,128]{1,0:T(8,128)S(1)}, u32[]{:S(2)}, u32[]{:S(2)}) %collective-permute-start) | collective-permute-done | bytes 786464 | tf_op jit(solution)/shard_map/ppermute | solution.py:559
  29.7 0.0 collective-permute-done.1.right
  29.7 3.4 %edge.1 = (f32[2,8,160,128]{3,2,1,0:T(8,128)S(1)}, f32[264,128]{1,0:T(8,128)S(1)}, f32[32,1024]{1,0:T(8,128)S(1)}, f32[1360,128]{1,0:T(8,128)S(1)}, f32[1360,128]{1,0:T(8,128)S(1)}, /*index=5*/f32[1360,128]{1,0:T(8,128)S(1)}) custom-call(s32[32]{0:T(128)S(1)} %concatenate.3.scal, f32[1536,128]{1,0:T(8,128)S(1)} %collective-permute-done.left, ...), custom_call_target="tpu_custom_call" | custom-call | bytes 18000000 | tf_op jit(solution)/shard_map/edge/pallas_call | solution.py:576
  33.2 2.5 %collective-permute-start.4 = (f32[264,128]{1,0:T(8,128)S(1)}, f32[264,128]{1,0:T(8,128)S(1)}, u32[]{:S(2)}, u32[]{:S(2)}) collective-permute-start(f32[264,128]{1,0:T(8,128)S(1)} %get-tuple-element.43), channel_id=1, source_target_pairs={{0,192},{32,224},{64,128},{96,160},{128,64},{160,96},{192,0},{224,... | collective-permute-start | bytes 405512 | tf_op jit(solution)/shard_map/ppermute | solution.py:527
  35.7 0.5 collective-permute-start.3
  36.2 0.3 collective-permute-start.2
  36.5 2.4 %flux.1.part = f32[8,128]{1,0:T(8,128)S(1)} custom-call(f32[2,8,160,128]{3,2,1,0:T(8,128)S(1)} %get-tuple-element.44.se, f32[8,768,128]{2,1,0:T(8,128)S(1)} %get-tuple-element.45.si, f32[1360,128]{1,0:T(8,128)S(1)} %get-tuple-element.34.aci.ac, f32[1360,128]{1,0:T(8,128)S(1)} %get-tuple-element.46.fx, f32[1360,128]{1,0:T(8,128)S(1)} %get-tuple-element.47.fy, ...), custom_call_target="tpu_custom_call" | custom-call | bytes 9000000 | tf_op jit(solution)/shard_map/flux/pallas_call | solution.py:587
  38.9 1.7 %collective-permute-done.4 = f32[264,128]{1,0:T(8,128)S(1)} collective-permute-done((f32[264,128]{1,0:T(8,128)S(1)}, f32[264,128]{1,0:T(8,128)S(1)}, u32[]{:S(2)}, u32[]{:S(2)}) %collective-permute-start.4) | collective-permute-done | bytes 135200 | tf_op jit(solution)/shard_map/ppermute | solution.py:527
  40.6 0.6 collective-permute-done.3
  41.2 0.4 collective-permute-done.2
  41.6 3.2 %collective-permute-start.5 = (f32[4,264,128]{2,1,0:T(8,128)S(1)}, f32[4,264,128]{2,1,0:T(8,128)S(1)}, u32[]{:S(2)}, u32[]{:S(2)}) collective-permute-start(f32[4,264,128]{2,1,0:T(8,128)S(1)} %pad_maximum_fusion.near), channel_id=1, source_target_pairs={{0,32},{32,0},{64,96},{96,64},{128,160},{160,128},{192,224},{224,1... | collective-permute-start | bytes 1622024 | tf_op jit(solution)/shard_map/ppermute | solution.py:527
  44.9 1.6 %collective-permute-done.5.far = f32[4,264,128]{2,1,0:T(8,128)S(1)} collective-permute-done((f32[4,264,128]{2,1,0:T(8,128)S(1)}, f32[4,264,128]{2,1,0:T(8,128)S(1)}, u32[]{:S(2)}, u32[]{:S(2)}) %collective-permute-start.5) | collective-permute-done | bytes 540704 | tf_op jit(solution)/shard_map/ppermute | solution.py:527
  46.4 1.2 %couple.1 = f32[32,8,128]{2,1,0:T(8,128)S(1)} custom-call(s32[32]{0:T(128)S(1)} %concatenate.3.scal, f32[32,1024]{1,0:T(8,128)S(1)} %get-tuple-element.42.window, f32[4,264,128]{2,1,0:T(8,128)S(1)} %pad_maximum_fusion.near, f32[4,264,128]{2,1,0:T(8,128)S(1)} %collective-permute-done.5.far, f32[8,128]{1,0:T(8,128)S(1)} %flux.1.part), custom_call_target="tpu_custom_call" | custom-call | bytes 3000000 | tf_op jit(solution)/shard_map/couple/pallas_call | solution.py:600
  47.6 16.2 %all_to_all.5.got = f32[32,8,128]{2,1,0:T(8,128)S(1)} all-to-all(f32[32,8,128]{2,1,0:T(8,128)S(1)} %couple.1), channel_id=1, replica_groups=mesh['subdomai'=8,'inner'=32] {'inner'}, dimensions={0} | all-to-all | bytes 262144 | tf_op jit(solution)/shard_map/all_to_all | solution.py:610
  63.8 4.9 %finish.1 = (f32[8,1024,128]{2,1,0:T(8,128)}, f32[8,8]{1,0:T(8,128)}, f32[6,8,8]{2,1,0:T(8,128)}) custom-call(s32[32]{0:T(128)S(1)} %concatenate.3.scal, f32[32,8,128]{2,1,0:T(8,128)S(1)} %all_to_all.5.got, f32[8,768,128]{2,1,0:T(8,128)S(1)} %get-tuple-element.45.si, f32[2,8,160,128]{3,2,1,0:T(8,128)S(1)} %get-tuple-element.44.se), custom_call_target="tpu_custom_call" | custom-call | bytes 15000000 | tf_op jit(solution)/shard_map/finish/pallas_call | solution.py:611
  (4 shorter events, 0.0 us)
Async XLA Ops:
  0.6 11.8 %copy-start.2 = (f32[16,64,128]{2,1,0:T(8,128)S(1)}, f32[16,64,128]{2,1,0:T(8,128)}, u32[]{:S(2)}) copy-start(f32[16,64,128]{2,1,0:T(8,128)} %param.8) | copy-start | bytes 1572868
  0.6 11.8 %copy-start.1 = (f32[16,64,128]{2,1,0:T(8,128)S(1)}, f32[16,64,128]{2,1,0:T(8,128)}, u32[]{:S(2)}) copy-start(f32[16,64,128]{2,1,0:T(8,128)} %param.7) | copy-start | bytes 1572868
  0.7 11.7 %copy-start.5 = (s32[1,6]{1,0:T(1,128)S(1)}, s32[1,6]{1,0:T(1,128)}, u32[]{:S(2)}) copy-start(s32[1,6]{1,0:T(1,128)} %param.11) | copy-start | bytes 76
  0.7 11.7 %copy-start.4 = (s32[1,6]{1,0:T(1,128)S(1)}, s32[1,6]{1,0:T(1,128)}, u32[]{:S(2)}) copy-start(s32[1,6]{1,0:T(1,128)} %param.10) | copy-start | bytes 76
  0.7 11.7 %copy-start.3 = (s32[1,2]{1,0:T(1,128)S(1)}, s32[1,2]{1,0:T(1,128)}, u32[]{:S(2)}) copy-start(s32[1,2]{1,0:T(1,128)} %param.9) | copy-start | bytes 28
  3.3 26.4 %collective-permute-start = (f32[1536,128]{1,0:T(8,128)}, f32[1536,128]{1,0:T(8,128)S(1)}, u32[]{:S(2)}, u32[]{:S(2)}) collective-permute-start(f32[1536,128]{1,0:T(8,128)} %get-tuple-element.30), channel_id=1, source_target_pairs={{0,1},{1,2},{2,3},{3,4},{4,5},{5,6},{6,7},{7,8},{8,9},{9,10},{10,1... | collective-permute-start | bytes 2359304 | tf_op jit(solution)/shard_map/ppermute | solution.py:559
  5.5 24.2 %collective-permute-start.1 = (f32[1536,128]{1,0:T(8,128)}, f32[1536,128]{1,0:T(8,128)S(1)}, u32[]{:S(2)}, u32[]{:S(2)}) collective-permute-start(f32[1536,128]{1,0:T(8,128)} %get-tuple-element.31), channel_id=1, source_target_pairs={{0,31},{1,0},{2,1},{3,2},{4,3},{5,4},{6,5},{7,6},{8,7},{9,8},{10,9... | collective-permute-start | bytes 2359304 | tf_op jit(solution)/shard_map/ppermute | solution.py:558
  12.5 2.2 %copy-start = (f32[8,16,64,128]{3,2,1,0:T(8,128)S(1)}, f32[8,16,64,128]{3,2,1,0:T(8,128)}, u32[]{:S(2)}) copy-start(f32[8,16,64,128]{3,2,1,0:T(8,128)} %param.6) | copy-start | bytes 12582916
  33.2 7.4 %collective-permute-start.4 = (f32[264,128]{1,0:T(8,128)S(1)}, f32[264,128]{1,0:T(8,128)S(1)}, u32[]{:S(2)}, u32[]{:S(2)}) collective-permute-start(f32[264,128]{1,0:T(8,128)S(1)} %get-tuple-element.43), channel_id=1, source_target_pairs={{0,192},{32,224},{64,128},{96,160},{128,64},{160,96},{192,0},{224,... | collective-permute-start | bytes 405512 | tf_op jit(solution)/shard_map/ppermute | solution.py:527
  35.7 5.5 %collective-permute-start.3 = (f32[264,128]{1,0:T(8,128)S(1)}, f32[264,128]{1,0:T(8,128)S(1)}, u32[]{:S(2)}, u32[]{:S(2)}) collective-permute-start(f32[264,128]{1,0:T(8,128)S(1)} %get-tuple-element.43), channel_id=1, source_target_pairs={{0,128},{32,160},{64,192},{96,224},{128,0},{160,32},{192,64},{224,... | collective-permute-start | bytes 405512 | tf_op jit(solution)/shard_map/ppermute | solution.py:527
  36.2 5.3 %collective-permute-start.2 = (f32[264,128]{1,0:T(8,128)S(1)}, f32[264,128]{1,0:T(8,128)S(1)}, u32[]{:S(2)}, u32[]{:S(2)}) collective-permute-start(f32[264,128]{1,0:T(8,128)S(1)} %get-tuple-element.43), channel_id=1, source_target_pairs={{0,64},{32,96},{64,0},{96,32},{128,192},{160,224},{192,128},{224,1... | collective-permute-start | bytes 405512 | tf_op jit(solution)/shard_map/ppermute | solution.py:527
  41.6 4.8 %collective-permute-start.5 = (f32[4,264,128]{2,1,0:T(8,128)S(1)}, f32[4,264,128]{2,1,0:T(8,128)S(1)}, u32[]{:S(2)}, u32[]{:S(2)}) collective-permute-start(f32[4,264,128]{2,1,0:T(8,128)S(1)} %pad_maximum_fusion.near), channel_id=1, source_target_pairs={{0,32},{32,0},{64,96},{96,64},{128,160},{160,128},{192,224},{224,1... | collective-permute-start | bytes 1622024 | tf_op jit(solution)/shard_map/ppermute | solution.py:527

commit v5 on v4

--- a/solution.py
+++ b/solution.py
@@ -583,7 +583,7 @@
         cost_estimate=cost(6),
         name="edge",
     )(scal, left, right, ve, kp, ac, fx, fy, fz, w, gram, first, window)
-    moved = [swap(sent, bits) for bits in (2, 4, 6)]
+    moved = [swap(sent, bits) for bits in (2, 6, 4)]
     part = pl.pallas_call(
         flux_kernel,
         out_shape=shape(8, CZ),
@@ -595,7 +595,7 @@
         name="flux",
     )(se, si, ac, fxe, fye, fze, flux)
     moved, part = lax.optimization_barrier((moved, part))
-    near = jnp.stack([sent] + moved)
+    near = jnp.stack([sent, moved[0], moved[2], moved[1]])
     far = swap(near, 1)
     msg = pl.pallas_call(
         couple_kernel,

time: 68.9 us -> 68.7 us (level)
  starting transfers between devices: 15.6 us -> 14.4 us
    ppermute x4, starting transfers between devices: 6.54 us -> 5.34 us  [swap(): lax.ppermute(x, 'subdomai', [(i, i ^ bits) for i in range(lax.axis_size('...]
  transfers between devices with their start and end apart: 6 -> 6, of which waited for: 5 -> 4; matrix products, arithmetic and copies ran while one was open for 0% -> 0% of each run, Pallas kernels for 24% -> 24%
where the time goes in v5:
time: 68.7 us; the launch traced here: 68.5 us
  Pallas kernels  28.7 us (42%)
  blocking collectives  16.8 us (24%)
  starting transfers between devices  14.4 us (21%)
  waiting for transfers between devices  5.64 us (8%)
  local copies, waits for them, and re-layouts  2.29 us (3%)
  between operations  0.75 us (1%)
    all_to_all x1, blocking collectives, body(): got = lax.all_to_all(msg, 'inner', 0, 0)  16.8 us
    pallas_call x1, Pallas kernels, body(): pl.pallas_call(interior_kernel, out_shape=(shape(K, INSIDE, CZ), shape(4,...  14.1 us
    ppermute x1, starting transfers between devices, body(): lax.ppermute(down, 'inner', [(i, (i - 1) % groups) for i in range(groups)])  6.82 us
    ppermute x4, starting transfers between devices, swap(): lax.ppermute(x, 'subdomai', [(i, i ^ bits) for i in range(lax.axis_size('...  5.34 us
    pallas_call x1, Pallas kernels, body(): pl.pallas_call(functools.partial(finish_kernel, 1.0 / cells), out_shape=(...  4.91 us
    ppermute x4, waiting for transfers between devices, swap(): lax.ppermute(x, 'subdomai', [(i, i ^ bits) for i in range(lax.axis_size('...  4.65 us
    pallas_call x1, Pallas kernels, body(): pl.pallas_call(edge_kernel, out_shape=(shape(2, K, EDGE, CZ), shape(SENT,...  3.44 us
    pallas_call x1, Pallas kernels, body(): pl.pallas_call(pack_kernel, out_shape=(shape(PACK, CZ),) * 2, in_specs=[H...  2.63 us
  transfers between devices with their start and end apart: 6, of which 4 were waited for; matrix products, arithmetic and copies ran while one was open for 0% of the time, Pallas kernels for 24%

profile of v5, /device:TPU:1, one launch (start us, length us, event | category | flops | bytes accessed | tf_op | source)
XLA Modules:
  0.0 68.5 jit_solution(13228318887887525506)
XLA Ops:
  0.6 0.0 copy-start.2
  0.6 0.0 copy-start.1
  0.7 0.0 copy-start.5
  0.7 0.0 copy-start.4
  0.7 0.0 copy-start.3
  0.7 2.6 %pack.1 = (f32[1536,128]{1,0:T(8,128)}, f32[1536,128]{1,0:T(8,128)}) custom-call(f32[8,1024,128]{2,1,0:T(8,128)} %bitcast.15, f32[1024,128]{1,0:T(8,128)} %bitcast.17, f32[1024,128]{1,0:T(8,128)} %bitcast.19), custom_call_target="tpu_custom_call" | custom-call | tf_op jit(solution)/shard_map/pack/pallas_call | solution.py:549
  3.3 2.2 %collective-permute-start = (f32[1536,128]{1,0:T(8,128)}, f32[1536,128]{1,0:T(8,128)S(1)}, u32[]{:S(2)}, u32[]{:S(2)}) collective-permute-start(f32[1536,128]{1,0:T(8,128)} %get-tuple-element.30), channel_id=1, source_target_pairs={{0,1},{1,2},{2,3},{3,4},{4,5},{5,6},{6,7},{7,8},{8,9},{9,10},{10,1... | collective-permute-start | bytes 2359304 | tf_op jit(solution)/shard_map/ppermute | solution.py:559
  5.5 6.8 %collective-permute-start.1 = (f32[1536,128]{1,0:T(8,128)}, f32[1536,128]{1,0:T(8,128)S(1)}, u32[]{:S(2)}, u32[]{:S(2)}) collective-permute-start(f32[1536,128]{1,0:T(8,128)} %get-tuple-element.31), channel_id=1, source_target_pairs={{0,31},{1,0},{2,1},{3,2},{4,3},{5,4},{6,5},{7,6},{8,7},{9,8},{10,9... | collective-permute-start | bytes 2359304 | tf_op jit(solution)/shard_map/ppermute | solution.py:558
  12.3 0.0 copy-done.5
  12.4 0.0 copy-done.4
  12.4 0.0 copy-done.3
  12.4 0.1 concatenate.3.scal
  12.5 0.0 copy-done.2
  12.5 0.0 copy-done.1
  12.5 0.0 copy-start
  12.5 2.2 %copy-done = f32[8,16,64,128]{3,2,1,0:T(8,128)S(1)} copy-done((f32[8,16,64,128]{3,2,1,0:T(8,128)S(1)}, f32[8,16,64,128]{3,2,1,0:T(8,128)}, u32[]{:S(2)}) %copy-start) | copy-done | bytes 4194328
  14.7 14.1 %interior.1 = (f32[8,768,128]{2,1,0:T(8,128)S(1)}, f32[4,8,128,128]{3,2,1,0:T(8,128)S(1)}, f32[1360,128]{1,0:T(8,128)S(1)}, f32[1360,128]{1,0:T(8,128)S(1)}, f32...) custom-call(s32[32]{0:T(128)S(1)} %concatenate.3.scal, ...), custom_call_target="tpu_custom_call" | custom-call | bytes 45000000 | tf_op jit(solution)/shard_map/interior/pallas_call | solution.py:563
  28.7 1.0 %collective-permute-done.left = f32[1536,128]{1,0:T(8,128)S(1)} collective-permute-done((f32[1536,128]{1,0:T(8,128)}, f32[1536,128]{1,0:T(8,128)S(1)}, u32[]{:S(2)}, u32[]{:S(2)}) %collective-permute-start) | collective-permute-done | bytes 786464 | tf_op jit(solution)/shard_map/ppermute | solution.py:559
  29.7 0.0 collective-permute-done.1.right
  29.7 3.4 %edge.1 = (f32[2,8,160,128]{3,2,1,0:T(8,128)S(1)}, f32[264,128]{1,0:T(8,128)S(1)}, f32[32,1024]{1,0:T(8,128)S(1)}, f32[1360,128]{1,0:T(8,128)S(1)}, f32[1360,128]{1,0:T(8,128)S(1)}, /*index=5*/f32[1360,128]{1,0:T(8,128)S(1)}) custom-call(s32[32]{0:T(128)S(1)} %concatenate.3.scal, f32[1536,128]{1,0:T(8,128)S(1)} %collective-permute-done.left, ...), custom_call_target="tpu_custom_call" | custom-call | bytes 18000000 | tf_op jit(solution)/shard_map/edge/pallas_call | solution.py:576
  33.2 2.8 %collective-permute-start.4 = (f32[264,128]{1,0:T(8,128)S(1)}, f32[264,128]{1,0:T(8,128)S(1)}, u32[]{:S(2)}, u32[]{:S(2)}) collective-permute-start(f32[264,128]{1,0:T(8,128)S(1)} %get-tuple-element.43), channel_id=1, source_target_pairs={{0,128},{32,160},{64,192},{96,224},{128,0},{160,32},{192,64},{224,... | collective-permute-start | bytes 405512 | tf_op jit(solution)/shard_map/ppermute | solution.py:527
  36.0 0.9 %collective-permute-start.3 = (f32[264,128]{1,0:T(8,128)S(1)}, f32[264,128]{1,0:T(8,128)S(1)}, u32[]{:S(2)}, u32[]{:S(2)}) collective-permute-start(f32[264,128]{1,0:T(8,128)S(1)} %get-tuple-element.43), channel_id=1, source_target_pairs={{0,192},{32,224},{64,128},{96,160},{128,64},{160,96},{192,0},{224,... | collective-permute-start | bytes 405512 | tf_op jit(solution)/shard_map/ppermute | solution.py:527
  36.8 0.0 collective-permute-start.2
  36.8 2.4 %flux.1.part = f32[8,128]{1,0:T(8,128)S(1)} custom-call(f32[2,8,160,128]{3,2,1,0:T(8,128)S(1)} %get-tuple-element.44.se, f32[8,768,128]{2,1,0:T(8,128)S(1)} %get-tuple-element.45.si, f32[1360,128]{1,0:T(8,128)S(1)} %get-tuple-element.34.aci.ac, f32[1360,128]{1,0:T(8,128)S(1)} %get-tuple-element.46.fx, f32[1360,128]{1,0:T(8,128)S(1)} %get-tuple-element.47.fy, ...), custom_call_target="tpu_custom_call" | custom-call | bytes 9000000 | tf_op jit(solution)/shard_map/flux/pallas_call | solution.py:587
  39.3 0.0 collective-permute-done.4
  39.3 2.8 %collective-permute-done.3 = f32[264,128]{1,0:T(8,128)S(1)} collective-permute-done((f32[264,128]{1,0:T(8,128)S(1)}, f32[264,128]{1,0:T(8,128)S(1)}, u32[]{:S(2)}, u32[]{:S(2)}) %collective-permute-start.3) | collective-permute-done | bytes 135200 | tf_op jit(solution)/shard_map/ppermute | solution.py:527
  42.1 0.2 collective-permute-done.2
  42.4 1.7 %collective-permute-start.5 = (f32[4,264,128]{2,1,0:T(8,128)S(1)}, f32[4,264,128]{2,1,0:T(8,128)S(1)}, u32[]{:S(2)}, u32[]{:S(2)}) collective-permute-start(f32[4,264,128]{2,1,0:T(8,128)S(1)} %pad_maximum_fusion.near), channel_id=1, source_target_pairs={{0,32},{32,0},{64,96},{96,64},{128,160},{160,128},{192,224},{224,1... | collective-permute-start | bytes 1622024 | tf_op jit(solution)/shard_map/ppermute | solution.py:527
  44.1 1.6 %collective-permute-done.5.far = f32[4,264,128]{2,1,0:T(8,128)S(1)} collective-permute-done((f32[4,264,128]{2,1,0:T(8,128)S(1)}, f32[4,264,128]{2,1,0:T(8,128)S(1)}, u32[]{:S(2)}, u32[]{:S(2)}) %collective-permute-start.5) | collective-permute-done | bytes 540704 | tf_op jit(solution)/shard_map/ppermute | solution.py:527
  45.7 1.2 %couple.1 = f32[32,8,128]{2,1,0:T(8,128)S(1)} custom-call(s32[32]{0:T(128)S(1)} %concatenate.3.scal, f32[32,1024]{1,0:T(8,128)S(1)} %get-tuple-element.42.window, f32[4,264,128]{2,1,0:T(8,128)S(1)} %pad_maximum_fusion.near, f32[4,264,128]{2,1,0:T(8,128)S(1)} %collective-permute-done.5.far, f32[8,128]{1,0:T(8,128)S(1)} %flux.1.part), custom_call_target="tpu_custom_call" | custom-call | bytes 3000000 | tf_op jit(solution)/shard_map/couple/pallas_call | solution.py:600
  46.8 16.8 %all_to_all.5.got = f32[32,8,128]{2,1,0:T(8,128)S(1)} all-to-all(f32[32,8,128]{2,1,0:T(8,128)S(1)} %couple.1), channel_id=1, replica_groups=mesh['subdomai'=8,'inner'=32] {'inner'}, dimensions={0} | all-to-all | bytes 262144 | tf_op jit(solution)/shard_map/all_to_all | solution.py:610
  63.6 4.9 %finish.1 = (f32[8,1024,128]{2,1,0:T(8,128)}, f32[8,8]{1,0:T(8,128)}, f32[6,8,8]{2,1,0:T(8,128)}) custom-call(s32[32]{0:T(128)S(1)} %concatenate.3.scal, f32[32,8,128]{2,1,0:T(8,128)S(1)} %all_to_all.5.got, f32[8,768,128]{2,1,0:T(8,128)S(1)} %get-tuple-element.45.si, f32[2,8,160,128]{3,2,1,0:T(8,128)S(1)} %get-tuple-element.44.se), custom_call_target="tpu_custom_call" | custom-call | bytes 15000000 | tf_op jit(solution)/shard_map/finish/pallas_call | solution.py:611
  (4 shorter events, 0.0 us)
Async XLA Ops:
  0.6 11.8 %copy-start.2 = (f32[16,64,128]{2,1,0:T(8,128)S(1)}, f32[16,64,128]{2,1,0:T(8,128)}, u32[]{:S(2)}) copy-start(f32[16,64,128]{2,1,0:T(8,128)} %param.8) | copy-start | bytes 1572868
  0.6 11.8 %copy-start.1 = (f32[16,64,128]{2,1,0:T(8,128)S(1)}, f32[16,64,128]{2,1,0:T(8,128)}, u32[]{:S(2)}) copy-start(f32[16,64,128]{2,1,0:T(8,128)} %param.7) | copy-start | bytes 1572868
  0.7 11.7 %copy-start.5 = (s32[1,6]{1,0:T(1,128)S(1)}, s32[1,6]{1,0:T(1,128)}, u32[]{:S(2)}) copy-start(s32[1,6]{1,0:T(1,128)} %param.11) | copy-start | bytes 76
  0.7 11.7 %copy-start.4 = (s32[1,6]{1,0:T(1,128)S(1)}, s32[1,6]{1,0:T(1,128)}, u32[]{:S(2)}) copy-start(s32[1,6]{1,0:T(1,128)} %param.10) | copy-start | bytes 76
  0.7 11.7 %copy-start.3 = (s32[1,2]{1,0:T(1,128)S(1)}, s32[1,2]{1,0:T(1,128)}, u32[]{:S(2)}) copy-start(s32[1,2]{1,0:T(1,128)} %param.9) | copy-start | bytes 28
  3.3 26.4 %collective-permute-start = (f32[1536,128]{1,0:T(8,128)}, f32[1536,128]{1,0:T(8,128)S(1)}, u32[]{:S(2)}, u32[]{:S(2)}) collective-permute-start(f32[1536,128]{1,0:T(8,128)} %get-tuple-element.30), channel_id=1, source_target_pairs={{0,1},{1,2},{2,3},{3,4},{4,5},{5,6},{6,7},{7,8},{8,9},{9,10},{10,1... | collective-permute-start | bytes 2359304 | tf_op jit(solution)/shard_map/ppermute | solution.py:559
  5.5 24.2 %collective-permute-start.1 = (f32[1536,128]{1,0:T(8,128)}, f32[1536,128]{1,0:T(8,128)S(1)}, u32[]{:S(2)}, u32[]{:S(2)}) collective-permute-start(f32[1536,128]{1,0:T(8,128)} %get-tuple-element.31), channel_id=1, source_target_pairs={{0,31},{1,0},{2,1},{3,2},{4,3},{5,4},{6,5},{7,6},{8,7},{9,8},{10,9... | collective-permute-start | bytes 2359304 | tf_op jit(solution)/shard_map/ppermute | solution.py:558
  12.5 2.2 %copy-start = (f32[8,16,64,128]{3,2,1,0:T(8,128)S(1)}, f32[8,16,64,128]{3,2,1,0:T(8,128)}, u32[]{:S(2)}) copy-start(f32[8,16,64,128]{3,2,1,0:T(8,128)} %param.6) | copy-start | bytes 12582916
  33.2 6.1 %collective-permute-start.4 = (f32[264,128]{1,0:T(8,128)S(1)}, f32[264,128]{1,0:T(8,128)S(1)}, u32[]{:S(2)}, u32[]{:S(2)}) collective-permute-start(f32[264,128]{1,0:T(8,128)S(1)} %get-tuple-element.43), channel_id=1, source_target_pairs={{0,128},{32,160},{64,192},{96,224},{128,0},{160,32},{192,64},{224,... | collective-permute-start | bytes 405512 | tf_op jit(solution)/shard_map/ppermute | solution.py:527
  36.0 6.2 %collective-permute-start.3 = (f32[264,128]{1,0:T(8,128)S(1)}, f32[264,128]{1,0:T(8,128)S(1)}, u32[]{:S(2)}, u32[]{:S(2)}) collective-permute-start(f32[264,128]{1,0:T(8,128)S(1)} %get-tuple-element.43), channel_id=1, source_target_pairs={{0,192},{32,224},{64,128},{96,160},{128,64},{160,96},{192,0},{224,... | collective-permute-start | bytes 405512 | tf_op jit(solution)/shard_map/ppermute | solution.py:527
  36.8 5.5 %collective-permute-start.2 = (f32[264,128]{1,0:T(8,128)S(1)}, f32[264,128]{1,0:T(8,128)S(1)}, u32[]{:S(2)}, u32[]{:S(2)}) collective-permute-start(f32[264,128]{1,0:T(8,128)S(1)} %get-tuple-element.43), channel_id=1, source_target_pairs={{0,64},{32,96},{64,0},{96,32},{128,192},{160,224},{192,128},{224,1... | collective-permute-start | bytes 405512 | tf_op jit(solution)/shard_map/ppermute | solution.py:527
  42.4 3.2 %collective-permute-start.5 = (f32[4,264,128]{2,1,0:T(8,128)S(1)}, f32[4,264,128]{2,1,0:T(8,128)S(1)}, u32[]{:S(2)}, u32[]{:S(2)}) collective-permute-start(f32[4,264,128]{2,1,0:T(8,128)S(1)} %pad_maximum_fusion.near), channel_id=1, source_target_pairs={{0,32},{32,0},{64,96},{96,64},{128,160},{160,128},{192,224},{224,1... | collective-permute-start | bytes 1622024 | tf_op jit(solution)/shard_map/ppermute | solution.py:527
